TPU v7x, 256 devices: a whole 4x4x8 slice. The times are simulated.
256 devices in a mesh: wide: 32 (over z, x), narrow: 8 (over y, core).
Axes of the slice: x: 4, y: 4, z: 8, core: 2. Of those that a mesh axis runs over, the one named last changes fastest.
Arguments:
- sar_feats: bfloat16 [32768, 1024], P(('wide', 'narrow')), may hold values from -16 to 16
- opt_feats: bfloat16 [32768, 1024], P(('wide', 'narrow')), may hold values from -16 to 16
- w_sar: bfloat16 [1024, 512], replicated, may hold values from -0.0625 to 0.0625
- w_opt: bfloat16 [1024, 512], replicated, may hold values from -0.0625 to 0.0625
- logit_scale: float32 [1], replicated, may hold values from 10 to 100
- partner: int32 [32768], P('wide'), may hold values from 0 to 32767, as said below
Outputs:
- loss: float32 [1], replicated
- grad_sar: bfloat16 [32768, 1024], P(('wide', 'narrow'))
- grad_opt: bfloat16 [32768, 1024], P(('wide', 'narrow'))
- grad_wsar: float32 [1024, 512], P(('wide', 'narrow'))
- grad_wopt: float32 [1024, 512], P(('wide', 'narrow'))
Inputs may be any that keep to these rules, and one draw needn't show every extreme that they name: Each optical image is the partner of exactly one radar image.
All inputs are finite; a program needn't handle non-finite values.
Results may differ from a plain program's by a relative error of at most 0.0095.
Values may be sent and summed in bfloat16 or wider, within the bound.
A program may use at most 128 MiB of HBM per device.

v0:
```python
import jax
import jax.numpy as jnp
from jax import lax
from jax.sharding import PartitionSpec as P


def project(features, weight):
    raw = jnp.dot(features, weight, preferred_element_type=jnp.float32)
    inverse = lax.rsqrt(jnp.sum(raw * raw, axis=1, keepdims=True) + 1e-06)
    return (raw, inverse, (raw * inverse).astype(jnp.bfloat16))


def unproject(features, weight, raw, inverse, grad_unit):
    inner = jnp.sum(raw * grad_unit, axis=1, keepdims=True)
    grad_raw = (inverse * grad_unit - raw * inverse * inverse * inverse * inner).astype(
        jnp.bfloat16
    )
    grad_feat = jnp.dot(grad_raw, weight.T, preferred_element_type=jnp.float32).astype(jnp.bfloat16)
    grad_weight = jnp.dot(features.T, grad_raw, preferred_element_type=jnp.float32)
    return (grad_feat, grad_weight)


def local(sar_feats, opt_feats, w_sar, w_opt, logit_scale, partner):
    factor = logit_scale[0]
    raw_s, inv_s, unit_s = project(sar_feats, w_sar)
    raw_o, inv_o, unit_o = project(opt_feats, w_opt)
    sar_block = lax.all_gather(unit_s, "narrow", axis=0, tiled=True)
    opt_block = lax.all_gather(unit_o, "wide", axis=0, tiled=True)
    own_rows = unit_s.shape[0]
    narrow_size = lax.axis_size("narrow")
    wide_size = lax.axis_size("wide")
    narrow_index = lax.axis_index("narrow")
    wide_index = lax.axis_index("wide")
    column = jnp.arange(opt_block.shape[0], dtype=jnp.int32)
    col_ids = (
        column // own_rows * (own_rows * narrow_size) + narrow_index * own_rows + column % own_rows
    )
    logits = factor * lax.dot_general(
        sar_block, opt_block, (((1,), (1,)), ((), ())), preferred_element_type=jnp.float32
    )
    mask = partner[:, None] == col_ids[None, :]
    masked = jnp.where(mask, logits, jnp.float32(0.0))
    row_max = lax.pmax(jnp.max(logits, axis=1), "narrow")
    col_max = lax.pmax(jnp.max(logits, axis=0), "wide")
    row_sum, pos_row = lax.psum(
        (jnp.sum(jnp.exp(logits - row_max[:, None]), axis=1), jnp.sum(masked, axis=1)), "narrow"
    )
    col_sum, pos_col = lax.psum(
        (jnp.sum(jnp.exp(logits - col_max[None, :]), axis=0), jnp.sum(masked, axis=0)), "wide"
    )
    lse_row = row_max + jnp.log(row_sum)
    lse_col = col_max + jnp.log(col_sum)
    gradient = (
        jnp.exp(logits - lse_row[:, None])
        + jnp.exp(logits - lse_col[None, :])
        - 2.0 * mask.astype(jnp.float32)
    ) * 0.5
    grad_logits = (factor * gradient).astype(jnp.bfloat16)
    sar_terms = jnp.dot(grad_logits, opt_block, preferred_element_type=jnp.float32)
    grad_us = lax.psum_scatter(sar_terms, "narrow", scatter_dimension=0, tiled=True)
    opt_terms = lax.dot_general(
        grad_logits, sar_block, (((0,), (0,)), ((), ())), preferred_element_type=jnp.float32
    )
    grad_uo = lax.psum_scatter(opt_terms, "wide", scatter_dimension=0, tiled=True)
    grad_sar, part_wsar = unproject(sar_feats, w_sar, raw_s, inv_s, grad_us)
    grad_opt, part_wopt = unproject(opt_feats, w_opt, raw_o, inv_o, grad_uo)
    grad_wsar, grad_wopt = (
        lax.psum_scatter(part_wsar, ("wide", "narrow"), scatter_dimension=0, tiled=True),
        lax.psum_scatter(part_wopt, ("wide", "narrow"), scatter_dimension=0, tiled=True),
    )
    row_terms = lax.dynamic_slice_in_dim(lse_row - pos_row, narrow_index * own_rows, own_rows, 0)
    col_terms = lax.dynamic_slice_in_dim(lse_col - pos_col, wide_index * own_rows, own_rows, 0)
    total = lax.psum(jnp.sum(row_terms) + jnp.sum(col_terms), ("wide", "narrow"))
    batch_rows = own_rows * wide_size * narrow_size
    loss = (total / (2.0 * batch_rows)).reshape(1)
    return (loss, grad_sar, grad_opt, grad_wsar, grad_wopt)


def solution(mesh):
    return jax.shard_map(
        local,
        mesh=mesh,
        in_specs=(
            P(("wide", "narrow"), None),
            P(("wide", "narrow"), None),
            P(),
            P(),
            P(),
            P("wide"),
        ),
        out_specs=(
            P(),
            P(("wide", "narrow"), None),
            P(("wide", "narrow"), None),
            P(("wide", "narrow"), None),
            P(("wide", "narrow"), None),
        ),
        check_vma=False,
    )
```

profile of v0, /device:TPU:1, one launch (start us, length us, event | category | flops | bytes accessed | tf_op | source)
XLA Modules:
  0.0 1017.9 jit_solution(9110033208592110157)
XLA Ops:
  7.2 1.2 copy-done
  8.4 1.3 multiply_reduce_fusion.5
  10.6 1.7 multiply_reduce_fusion.4
  13.8 27.0 %all-gather.3.cloned.1.call-done = bf16[1024,512]{1,0:T(8,128)(2,1)} async-done(((bf16[128,512]{1,0:T(8,128)(2,1)}), bf16[1024,512]{1,0:T(8,128)(2,1)}) %all-gather.3.cloned.1.call-update) | async-done | bytes 1048592 | tf_op jit(solution)/shard_map/all_gather | solution.py:27
  40.8 81.8 %all-gather.5.cloned.1.call-done = bf16[4096,512]{1,0:T(8,128)(2,1)} async-done(((bf16[128,512]{1,0:T(8,128)(2,1)}), bf16[4096,512]{1,0:T(8,128)(2,1)}) %all-gather.5.cloned.1.call-update) | async-done | bytes 4194320 | tf_op jit(solution)/shard_map/all_gather | solution.py:28
  122.6 12.8 %multiply_reduce_fusion = (f32[4096]{0:T(1024)S(1)}, f32[1024]{0:T(1024)S(1)}, f32[1024,4096]{1,0:T(8,128)}) fusion(f32[]{:T(128)} %bitcast.28, bf16[1024,512]{1,0:T(8,128)(2,1)} %all-gather.3.cloned.1.call-done, bf16[4096,512]{1,0:T(8,128)(2,1)} %all-gather.5.cloned.1.call-done), kind=kOutput, calls=%fused_computation.9 | convolution fusion | flops 4307545088 | bytes 22040580 | tf_op jit(solution)/shard_map/dot_general | solution.py:38
  135.4 111.8 %pmax.15 = f32[4096]{0:T(1024)S(1)} all-reduce(f32[4096]{0:T(1024)S(1)} %get-tuple-element.21), channel_id=1, replica_groups=mesh['wide'=32,'narrow'=8] {'wide'}, use_global_device_ids=true, to_apply=%region_10.11 | all-reduce | flops 4096 | bytes 32768 | tf_op jit(solution)/shard_map/pmax | solution.py:44
  247.2 43.8 %pmax.14 = f32[1024]{0:T(1024)S(1)} all-reduce(f32[1024]{0:T(1024)S(1)} %get-tuple-element.22), channel_id=1, replica_groups=mesh['wide'=32,'narrow'=8] {'narrow'}, use_global_device_ids=true, to_apply=%region_3.4 | all-reduce | flops 1024 | bytes 8192 | tf_op jit(solution)/shard_map/pmax | solution.py:43
  291.0 11.4 %exponential_reduce_fusion = (f32[4096]{0:T(1024)S(1)}, f32[1024]{0:T(1024)S(1)}, f32[1024]{0:T(1024)S(1)}, f32[4096]{0:T(1024)S(1)}) fusion(f32[1024,4096]{1,0:T(8,128)} %get-tuple-element.35, f32[4096]{0:T(1024)S(1)} %pmax.15, f32[]{:T(128)} %bitcast.31, f32[1024]{0:T(1024)S(1)} %pmax.14, s32[4096]{0:T(1024)S(1)} %fusion.13, s32[1024]{0:T(1024)S(1)} %copy-done.5), kind=kLoop, calls=%fused_computation.5 | loop fusion | flops 37738496 | bytes 16859140 | tf_op jit(solution)/shard_map/reduce_sum | solution.py:49
  302.4 109.9 %all-reduce.3 = (f32[4096]{0:T(1024)S(1)}, f32[4096]{0:T(1024)S(1)}) all-reduce(f32[4096]{0:T(1024)S(1)} %get-tuple-element.20, f32[4096]{0:T(1024)S(1)} %get-tuple-element.17), channel_id=1, replica_groups=mesh['wide'=32,'narrow'=8] {'wide'}, use_global_device_ids=true, to_apply=%region_14.15 | all-reduce | flops 8192 | bytes 65536 | tf_op jit(solution)/shard_map/psum | solution.py:48
  412.3 40.6 %all-reduce.4 = (f32[1024]{0:T(1024)S(1)}, f32[1024]{0:T(1024)S(1)}) all-reduce(f32[1024]{0:T(1024)S(1)} %get-tuple-element.18, f32[1024]{0:T(1024)S(1)} %get-tuple-element.19), channel_id=1, replica_groups=mesh['wide'=32,'narrow'=8] {'narrow'}, use_global_device_ids=true, to_apply=%region_5.6 | all-reduce | flops 2048 | bytes 16384 | tf_op jit(solution)/shard_map/psum | solution.py:45
  452.9 10.2 %fusion.2 = bf16[1024,4096]{1,0:T(8,128)(2,1)S(1)} fusion(f32[1024,4096]{1,0:T(8,128)} %get-tuple-element.35, f32[]{:T(128)S(6)} %mul.141, f32[4096]{0:T(1024)S(1)} %log_add_fusion, f32[1024]{0:T(1024)S(1)} %get-tuple-element.30, s32[4096]{0:T(1024)S(1)} %fusion.13, f32[]{:T(128)} %bitcast.30, s32[1024]{0:T(1024)S(1)} %copy-done.5), kind=kLoop, calls=%fused_computation.4 | loop fusion | flops 37748736 | bytes 25206792 | tf_op jit(solution)/shard_map/convert_element_type | solution.py:58
  463.1 3.2 copy-done.1
  466.4 5.8 fusion.17
  472.3 10.4 %fusion.18 = f32[4096,512]{1,0:T(8,128)} fusion(bf16[1024,4096]{1,0:T(8,128)(2,1)} %copy-done.1, bf16[1024,512]{1,0:T(8,128)(2,1)S(1)} %copy-done.7), kind=kOutput, calls=%fused_computation.48 | convolution fusion | flops 4294967296 | bytes 17825792 | tf_op jit(solution)/shard_map/dot_general | solution.py:61
  482.8 17.3 %reduce-scatter.5.cloned.1.call-done = f32[128,512]{1,0:T(8,128)} async-done(((f32[1024,512]{1,0:T(8,128)}), f32[128,512]{1,0:T(8,128)}) %reduce-scatter.5.cloned.1.call-update) | async-done | bytes 262160 | tf_op jit(solution)/shard_map/reduce_scatter | solution.py:60
  502.3 1.8 convolution_bitcast_fusion.1
  504.1 226.6 %reduce-scatter.7.cloned.1.call-done = f32[128,512]{1,0:T(8,128)} async-done(((f32[4096,512]{1,0:T(8,128)}), f32[128,512]{1,0:T(8,128)}) %reduce-scatter.7.cloned.1.call-update) | async-done | bytes 262160 | tf_op jit(solution)/shard_map/reduce_scatter | solution.py:64
  732.9 1.8 convolution_bitcast_fusion
  737.3 78.7 %psum.39 = f32[]{:T(128)} all-reduce(f32[]{:T(128)S(6)} %add.94), channel_id=1, replica_groups=mesh['wide'=32,'narrow'=8] {'wide','narrow'}, use_global_device_ids=true, to_apply=%region_16.17 | all-reduce | flops 1 | bytes 8 | tf_op jit(solution)/shard_map/psum | solution.py:73
  816.7 1.2 convolution_convert_fusion.1
  817.9 1.2 convolution_convert_fusion
  819.0 188.5 %all-reduce.7.cloned.1.call-done = (f32[1024,512]{0,1:T(8,128)}, f32[1024,512]{0,1:T(8,128)}) async-done(((f32[1024,512]{0,1:T(8,128)}, f32[1024,512]{0,1:T(8,128)}), (f32[1024,512]{0,1:T(8,128)}, f32[1024,512]{0,1:T(8,128)})) %all-reduce.7.cloned.1.call-update) | async-done | bytes 4194320
  1007.6 1.2 constant_dynamic-slice_fusion
  (39 shorter events, 8.9 us)
Async XLA Ops:
  7.2 1.2 copy-start
  7.2 283.8 %copy-start.5 = (s32[1024]{0:T(1024)S(1)}, s32[1024]{0:T(1024)}, u32[]{:S(2)}) copy-start(s32[1024]{0:T(1024)} %param.11) | copy-start | bytes 12292
  7.2 33.7 %all-gather.3.cloned.1.call-start = ((), (), s32[]{:S(2)}) async-start(), calls=%async_computation.2 | async-start | bytes 1179648 | tf_op jit(solution)/shard_map/all_gather | solution.py:27
  10.5 112.1 %all-gather.5.cloned.1.call-start = ((), (), s32[]{:S(2)}) async-start(), calls=%async_computation.3 | async-start | bytes 4325376 | tf_op jit(solution)/shard_map/all_gather | solution.py:28
  13.1 487.1 %reduce-scatter.5.cloned.1.call-start = ((), (), s32[]{:S(2)}) async-start(), calls=%async_computation.4 | async-start | bytes 2359296 | tf_op jit(solution)/shard_map/reduce_scatter | solution.py:60
  452.9 13.5 %copy-start.6 = (bf16[4096,512]{1,0:T(8,128)(2,1)S(1)}, bf16[4096,512]{1,0:T(8,128)(2,1)}, u32[]{:S(2)}) copy-start(bf16[4096,512]{1,0:T(8,128)(2,1)} %all-gather.5.cloned.1.call-done) | copy-start | bytes 12582916
  463.1 3.2 copy-start.1
  466.4 5.9 copy-start.7
  472.2 30.1 %copy-start.3 = (bf16[128,1024]{1,0:T(8,128)(2,1)S(1)}, bf16[128,1024]{1,0:T(8,128)(2,1)}, u32[]{:S(2)}) copy-start(bf16[128,1024]{1,0:T(8,128)(2,1)} %param.6) | copy-start | bytes 786436
  472.2 260.6 %copy-start.4 = (bf16[128,1024]{1,0:T(8,128)(2,1)S(1)}, bf16[128,1024]{1,0:T(8,128)(2,1)}, u32[]{:S(2)}) copy-start(bf16[128,1024]{1,0:T(8,128)(2,1)} %param.7) | copy-start | bytes 786436
  472.2 258.5 %reduce-scatter.7.cloned.1.call-start = ((), (), s32[]{:S(2)}) async-start(), calls=%async_computation.5 | async-start | bytes 8650752 | tf_op jit(solution)/shard_map/reduce_scatter | solution.py:64
  482.7 335.1 %copy-start.2 = (bf16[1024,512]{1,0:T(8,128)(2,1)S(1)}, bf16[1024,512]{1,0:T(8,128)(2,1)}, u32[]{:S(2)}) copy-start(bf16[1024,512]{1,0:T(8,128)(2,1)} %param.9) | copy-start | bytes 3145732
  482.7 524.8 %all-reduce.7.cloned.1.call-start = ((), (), s32[]{:S(2)}) async-start(), calls=%async_computation.6 | async-start | bytes 8388608
Sparse Core Ops, SparseCore 0:
  10.6 30.1 all-gather.2
  44.0 78.5 all-gather.4
  472.3 27.7 reduce-scatter.4
  504.0 226.6 reduce-scatter.6
  737.1 270.3 all-reduce.6
where the time goes:
time: 1020 us
  waiting for transfers between devices  541 us (53%)
  blocking collectives  385 us (38%)
  matrix products  38.1 us (4%)
  other arithmetic  28.8 us (3%)
  between operations  17.7 us (2%)
    reduce_scatter x1, waiting for transfers between devices, local(): lax.psum_scatter(opt_terms, 'wide', scatter_dimension=0, tiled=True)  227 us
    unnamed x6, waiting for transfers between devices  189 us
    pmax x1, blocking collectives, local(): col_max = lax.pmax(jnp.max(logits, axis=0), 'wide')  112 us
    psum x1, blocking collectives, local(): lax.psum((jnp.sum(jnp.exp(logits - col_max[None, :]), axis=0), jnp.sum(ma...  110 us
    all_gather x1, waiting for transfers between devices, local(): opt_block = lax.all_gather(unit_o, 'wide', axis=0, tiled=True)  81.8 us
    psum x1, blocking collectives, local(): lax.psum(jnp.sum(row_terms) + jnp.sum(col_terms), ('wide', 'narrow'))  78.7 us
    pmax x1, blocking collectives, local(): row_max = lax.pmax(jnp.max(logits, axis=1), 'narrow')  43.8 us
    psum x1, blocking collectives, local(): lax.psum((jnp.sum(jnp.exp(logits - row_max[:, None]), axis=1), jnp.sum(ma...  40.6 us
  transfers between devices with their start and end apart: 5, of which 5 were waited for; matrix products, arithmetic and copies ran while one was open for 2% of the time, Pallas kernels for 0%

commit v1 on v0

v1 whole, which is shorter than its diff:
```python
import jax
import jax.numpy as jnp
from jax import lax
from jax.experimental import pallas as pl
from jax.experimental.pallas import tpu as pltpu
from jax.sharding import PartitionSpec as P

NX, NY, NZ = 4, 4, 8
R = 128
E = 512
F = 1024
HALF = 256
TR = NZ * 2 * R
TC = NX * NY * R
LOG2E = 1.4426950408889634
SHIFT = 25.0
MSGS = 240
f32 = jnp.float32
bf16 = jnp.bfloat16
MESH = pl.DeviceIdType.MESH


def dot_nt(a, b):
    return lax.dot_general(a, b, (((1,), (1,)), ((), ())), preferred_element_type=f32)


def dot_nn(a, b):
    return jnp.dot(a, b, preferred_element_type=f32)


def kernel(
    sar_ref, opt_ref, ws_ref, wo_ref, scale_ref, partner_ref,
    loss_ref, gsar_ref, gopt_ref, gws_ref, gwo_ref,
    a_ref, at_ref, b_ref, e_ref, g_ref, raws_ref, rawo_ref,
    part_ref, prow_ref, cid_ref, racc_ref, cacc_ref, pacc_ref,
    rsnd_ref, csnd_ref, rrcv_ref, crcv_ref, rst_ref, cst_ref, rrow_ref,
    acc_ref, gbt_ref, rh0_ref, rh1_ref, th0_ref, th1_ref, p2h0_ref, p2h1_ref,
    qown_ref, qsis_ref, qrcv_ref, qsnd_ref, zp0_ref, zm0_ref, zp_ref, zm_ref,
    fsnd_ref, frcv_ref, ft_ref, gmine_ref, gsnd_ref, grcv_ref, w_ref,
    sx_ref, sy_ref, rx_ref, ry_ref, sx2_ref, sy2_ref, rx2_ref, ry2_ref,
    u_ref, rz_ref, fin_ref, sis_ref, lr_ref,
    ssem, rsem,
):
    wide = lax.axis_index("wide")
    narrow = lax.axis_index("narrow")
    x, y, z, c = lax.rem(wide, NX), narrow // 2, wide // NX, lax.rem(narrow, 2)

    def dev(dx=0, dy=0, dz=0, dc=0):
        px = lax.rem(x + (dx % NX), NX)
        py = lax.rem(y + (dy % NY), NY)
        pz = lax.rem(z + (dz % NZ), NZ)
        pc = lax.rem(c + (dc % 2), 2)
        return (pz * NX + px, py * 2 + pc)

    plane = [(i, j) for i in range(NX) for j in range(NY) if (i, j) != (0, 0)]
    zcs = [(i, j) for i in range(NZ) for j in range(2) if (i, j) != (0, 0)]

    barrier = pltpu.get_barrier_semaphore()
    for i, j in plane:
        pl.semaphore_signal(barrier, inc=1, device_id=dev(dx=i, dy=j), device_id_type=MESH)
    for i, j in zcs:
        pl.semaphore_signal(barrier, inc=1, device_id=dev(dz=i, dc=j), device_id_type=MESH)

    sent = []

    def send(src, dst, device):
        m = len(sent)
        copy = pltpu.make_async_remote_copy(
            src_ref=src, dst_ref=dst, send_sem=ssem.at[m], recv_sem=rsem.at[m],
            device_id=device, device_id_type=MESH,
        )
        copy.start()
        sent.append(copy)
        return copy

    def brow(dx, dy):
        return ((dx % NX) * NY + (dy % NY)) * R

    def arow(dz, dc):
        return ((dz % NZ) * 2 + dc % 2) * R

    scale = scale_ref[0]

    def project(feat_ref, w_ref, raw_ref, dst_ref):
        raw = dot_nn(feat_ref[...], w_ref[...])
        inv = lax.rsqrt(jnp.sum(raw * raw, axis=1, keepdims=True) + 1e-06)
        raw_ref[...] = raw
        dst_ref[pl.ds(0, R), :] = (raw * inv).astype(bf16)
        return inv

    inv_o = project(opt_ref, wo_ref, rawo_ref, b_ref)
    inv_s = project(sar_ref, ws_ref, raws_ref, a_ref)
    own_partner = partner_ref[pl.ds(narrow, 1), :].astype(f32)
    part_ref[0] = jnp.broadcast_to(own_partner, (8, R))
    core0 = c == 0
    sar = sar_ref[...]
    opt = opt_ref[...]
    fsnd_ref[...] = jnp.where(core0, opt, sar)

    pl.semaphore_wait(barrier, len(plane) + len(zcs))

    bx, by, az = {}, {}, {}
    own_b = b_ref.at[pl.ds(0, R)]
    own_a = a_ref.at[pl.ds(0, R)]
    up = send(own_a, a_ref.at[pl.ds(arow(-1, 0), R)], dev(dz=1))
    down = send(own_a, a_ref.at[pl.ds(arow(1, 0), R)], dev(dz=-1))
    for d in (1, 3, 2):
        bx[d] = send(own_b, b_ref.at[pl.ds(brow(-d, 0), R)], dev(dx=d))
        by[d] = send(own_b, b_ref.at[pl.ds(brow(0, -d), R)], dev(dy=d))
    sister = [send(own_a, a_ref.at[pl.ds(arow(0, 1), R)], dev(dc=1))]
    parts = [
        send(part_ref.at[0], part_ref.at[((-i) % NZ) * 2 + j], dev(dz=i, dc=j)) for i, j in zcs
    ]
    fcopy = send(fsnd_ref, frcv_ref, dev(dc=1))

    ft_ref[:, pl.ds(0, R)] = jnp.where(core0, sar, opt).T
    lane = lax.broadcasted_iota(jnp.int32, (8, R), 1)
    for i in range(NX):
        for j in range(NY):
            wx = z * NX + lax.rem(x + i, NX)
            ny = lax.rem(y + j, NY) * 2 + c
            base = (wx * (NY * 2) + ny) * R
            cid_ref[:, pl.ds(brow(i, j), R)] = (lane + base).astype(f32)

    def transpose_a(row):
        at_ref[:, pl.ds(row, R)] = a_ref[pl.ds(row, R), :].T

    transpose_a(0)

    late = []
    for d in (1, 3, 2):
        bx[d].wait_recv()
        blk = b_ref.at[pl.ds(brow(-d, 0), R), pl.ds(0, HALF)]
        for dy in (1, 3, 2):
            late.append(send(
                blk, b_ref.at[pl.ds(brow(-d, -dy), R), pl.ds(0, HALF)], dev(dy=dy)))
        by[d].wait_recv()
        blk = b_ref.at[pl.ds(brow(0, -d), R), pl.ds(HALF, HALF)]
        for dx in (1, 3, 2):
            late.append(send(
                blk, b_ref.at[pl.ds(brow(-dx, -d), R), pl.ds(HALF, HALF)], dev(dx=dx)))
        up.wait_recv()
        blk = a_ref.at[pl.ds(arow(-len(sister), 0), R)]
        down.wait_recv()
        blk2 = a_ref.at[pl.ds(arow(len(sister), 0), R)]
        s = len(sister)
        if s < 3:
            up = send(blk, a_ref.at[pl.ds(arow(-s - 1, 0), R)], dev(dz=1))
            down = send(blk2, a_ref.at[pl.ds(arow(s + 1, 0), R)], dev(dz=-1))
        else:
            up = send(
                blk.at[:, pl.ds(0, HALF)],
                a_ref.at[pl.ds(arow(4, 0), R), pl.ds(0, HALF)], dev(dz=1))
            down = send(
                blk2.at[:, pl.ds(HALF, HALF)],
                a_ref.at[pl.ds(arow(4, 0), R), pl.ds(HALF, HALF)], dev(dz=-1))
        late.append(send(blk, a_ref.at[pl.ds(arow(-s, 1), R)], dev(dc=1)))
        late.append(send(blk2, a_ref.at[pl.ds(arow(s, 1), R)], dev(dc=1)))
        sister.append(None)
        transpose_a(arow(-s, 0))
        transpose_a(arow(s, 0))
    up.wait_recv()
    down.wait_recv()
    late.append(send(
        a_ref.at[pl.ds(arow(4, 0), R)], a_ref.at[pl.ds(arow(4, 1), R)], dev(dc=1)))
    transpose_a(arow(4, 0))
    for copy in parts:
        copy.wait_recv()
    for q in range(NZ * 2):
        prow_ref[pl.ds(q * R, R), :] = jnp.broadcast_to(part_ref[q][0:1, :], (R, R)).T
    fcopy.wait_recv()
    ft_ref[:, pl.ds(R, R)] = frcv_ref[...].T
    sister[0].wait_recv()
    for copy in late:
        copy.wait_recv()
    for d in range(NZ):
        transpose_a(arow(d, 1))

    mul = scale * (0.5 * LOG2E)
    up_factor = 5.184705528587072e21
    cacc_ref[...] = jnp.zeros_like(cacc_ref)
    CH = 32

    @pl.loop(0, NZ)
    def _(rb):
        r0 = pl.multiple_of(rb * HALF, HALF)
        a_blk = a_ref[pl.ds(r0, HALF), :]
        for sl in range(NX):
            e_ref[sl, pl.ds(r0, HALF), :] = dot_nt(a_blk, b_ref[pl.ds(sl * E, E), :])
        for sl in range(NX):
            c1 = jnp.zeros((8, E), f32)
            c2 = jnp.zeros((8, E), f32)
            for ch in range(HALF // CH):
                rows = pl.ds(pl.multiple_of(r0 + ch * CH, CH), CH)
                e = jnp.exp2(e_ref[sl, rows, :] * mul - SHIFT * LOG2E)
                e_ref[sl, rows, :] = e
                q1 = e * e
                u = e * up_factor
                q2 = u * u
                c1 = c1 + jnp.sum(q1.reshape(CH // 8, 8, E), axis=0)
                c2 = c2 + jnp.sum(q2.reshape(CH // 8, 8, E), axis=0)
                r1 = (q1[:, 0:128] + q1[:, 128:256]) + (q1[:, 256:384] + q1[:, 384:512])
                r2 = (q2[:, 0:128] + q2[:, 128:256]) + (q2[:, 256:384] + q2[:, 384:512])
                if sl > 0:
                    r1 = r1 + racc_ref[0, rows, :]
                    r2 = r2 + racc_ref[1, rows, :]
                racc_ref[0, rows, :] = r1
                racc_ref[1, rows, :] = r2
            cols = pl.ds(sl * E, E)
            cacc_ref[0, :, cols] += c1
            cacc_ref[1, :, cols] += c2

    ones = jnp.full((8, R), 0.125, bf16)
    rmsg, cmsg = [], []
    for i, j in [(0, 0)] + zcs:
        q = i * 2 + j
        for k in range(2):
            v = racc_ref[k, pl.ds(q * R, R), :]
            hi = v.astype(bf16)
            lo = (v - hi.astype(f32)).astype(bf16)
            rsnd_ref[q, pl.ds(8 * k, 8), :] = dot_nt(ones, hi) + dot_nt(ones, lo)
        if q:
            rmsg.append(send(rsnd_ref.at[q], rrcv_ref.at[q], dev(dz=i, dc=j)))
    for i, j in [(0, 0)] + plane:
        p = i * NY + j
        for k in range(2):
            csnd_ref[p, pl.ds(8 * k, 8), :] = cacc_ref[k, :, pl.ds(p * R, R)]
        if p:
            cmsg.append(send(csnd_ref.at[p], crcv_ref.at[p], dev(dx=i, dy=j)))

    half_scale = scale * 0.5

    def finish(total):
        s1 = jnp.sum(total[0:8], axis=0, keepdims=True)
        s2 = jnp.sum(total[8:16], axis=0, keepdims=True)
        lse = jnp.where(
            s1 > 1.9287498e-22, jnp.log(s1) + 2.0 * SHIFT, jnp.log(s2) - 2.0 * SHIFT)
        factor = jnp.exp(SHIFT - 0.5 * lse) * jnp.sqrt(jnp.full((1, R), half_scale, f32))
        return lse, jnp.broadcast_to(factor, (8, R))

    total = rsnd_ref[0]
    for n, copy in enumerate(rmsg):
        copy.wait_recv()
        total = total + rrcv_ref[n + 1]
    lse_row, factor = finish(total)
    rst_ref[0] = factor
    rmsg = [
        send(rst_ref.at[0], rst_ref.at[((-i) % NZ) * 2 + j], dev(dz=i, dc=j)) for i, j in zcs
    ]
    total = csnd_ref[0]
    for n, copy in enumerate(cmsg):
        copy.wait_recv()
        total = total + crcv_ref[n + 1]
    lse_col, factor = finish(total)
    cst_ref[:, pl.ds(0, R)] = factor
    cmsg = [
        send(cst_ref.at[:, pl.ds(0, R)], cst_ref.at[:, pl.ds(brow(-i, -j), R)], dev(dx=i, dy=j))
        for i, j in plane
    ]
    rrow_ref[pl.ds(0, R), :] = jnp.broadcast_to(rst_ref[0][0:1, :], (R, R)).T
    for (i, j), copy in zip(zcs, rmsg):
        copy.wait_recv()
        q = ((-i) % NZ) * 2 + j
        rrow_ref[pl.ds(q * R, R), :] = jnp.broadcast_to(rst_ref[q][0:1, :], (R, R)).T
    for copy in cmsg:
        copy.wait_recv()

    h0, h1 = {}, {}
    for n, sl in enumerate((2, 1, 3, 0)):
        acc_ref[...] = jnp.zeros_like(acc_ref)

        @pl.loop(0, NZ)
        def _(rb):
            r0 = pl.multiple_of(rb * HALF, HALF)
            for ch in range(HALF // CH):
                rows = pl.ds(pl.multiple_of(r0 + ch * CH, CH), CH)
                rr = rrow_ref[rows, :].reshape(CH // 8, 8, R)
                pr = prow_ref[rows, :].reshape(CH // 8, 8, R)
                pos = None
                for lg in range(NY):
                    lanes = pl.ds(lg * R, R)
                    e = e_ref[sl, rows, lanes].reshape(CH // 8, 8, R)
                    cols = pl.ds(sl * E + lg * R, R)
                    u = e * rr
                    v = e * cst_ref[:, cols][None]
                    hit = pr == cid_ref[:, cols][None]
                    g = u * u + v * v - jnp.where(hit, scale, 0.0)
                    pe = jnp.where(hit, e, 0.0)
                    pos = pe if pos is None else pos + pe
                    g_ref[sl, rows, lanes] = g.reshape(CH, R).astype(bf16)
                pos = pos.reshape(CH, R)
                if n > 0:
                    pos = pos + pacc_ref[rows, :]
                pacc_ref[rows, :] = pos
            acc_ref[...] += dot_nn(
                at_ref[:, pl.ds(r0, HALF)], g_ref[sl, pl.ds(r0, HALF), :])

        gbt_ref[sl] = acc_ref[...].astype(bf16)
        if sl:
            h0[sl] = send(gbt_ref.at[sl, pl.ds(0, HALF)], rh0_ref.at[sl - 1], dev(dx=sl))
        for dy in (2, 1, 3):
            h1[sl, dy] = send(
                gbt_ref.at[sl, pl.ds(HALF, HALF), pl.ds(dy * R, R)],
                rh1_ref.at[dy - 1, sl], dev(dy=dy))

    qmsg = {}

    def radar(d):
        total = None
        for sl in range(NX):
            t = dot_nn(g_ref[sl, pl.ds(arow(d, 0), HALF), :], b_ref[pl.ds(sl * E, E), :])
            total = t if total is None else total + t
        qown_ref[d % NZ] = total[0:R]
        qsis_ref[d % NZ] = total[R:].astype(bf16)
        qmsg[d] = send(qsis_ref.at[d % NZ], qrcv_ref.at[d % NZ], dev(dc=1))

    def chip_sum(d):
        qmsg[d].wait_recv()
        return qown_ref[d % NZ] + qrcv_ref[d % NZ].astype(f32)

    def ring(d, sign, prev):
        q = chip_sum(d)
        k = abs(d)
        if k == 3:
            prev.wait_recv()
            if sign > 0:
                left = q[:, :HALF] + zp0_ref[...].astype(f32)
                qsnd_ref[d % NZ, :, pl.ds(0, HALF)] = left.astype(bf16)
                qsnd_ref[d % NZ, :, pl.ds(HALF, HALF)] = q[:, HALF:].astype(bf16)
            else:
                right = q[:, HALF:] + zm0_ref[...].astype(f32)
                qsnd_ref[d % NZ, :, pl.ds(0, HALF)] = q[:, :HALF].astype(bf16)
                qsnd_ref[d % NZ, :, pl.ds(HALF, HALF)] = right.astype(bf16)
        else:
            prev.wait_recv()
            inc = zp_ref if sign > 0 else zm_ref
            qsnd_ref[d % NZ] = (q + inc[2 - k].astype(f32)).astype(bf16)
        dst = zp_ref if sign > 0 else zm_ref
        return send(qsnd_ref.at[d % NZ], dst.at[3 - k], dev(dz=sign))

    radar(4)
    radar(3)
    qsnd_ref[4] = chip_sum(4).astype(bf16)
    zp = send(qsnd_ref.at[4, :, pl.ds(0, HALF)], zp0_ref, dev(dz=1))
    zm = send(qsnd_ref.at[4, :, pl.ds(HALF, HALF)], zm0_ref, dev(dz=-1))
    radar(-3)
    radar(2)
    radar(-2)
    zp = ring(3, 1, zp)
    zm = ring(-3, -1, zm)
    radar(1)
    radar(-1)
    radar(0)

    pos = pacc_ref[...]
    pos = jnp.where(pos > 0.0, 2.0 * (jnp.log(jnp.where(pos > 0.0, pos, 1.0)) + SHIFT), 0.0)
    pos = jnp.sum(pos.reshape(TR // 8, 8, R), axis=0)
    row0 = lax.broadcasted_iota(jnp.int32, (8, R), 0) == 0
    both = jnp.broadcast_to(lse_row + lse_col, (8, R))
    lr_ref[0] = jnp.where(row0, both, 0.0) - 2.0 * pos
    lmsg = [send(lr_ref.at[0], lr_ref.at[NX - d], dev(dx=d)) for d in range(1, NX)]

    zp = ring(2, 1, zp)
    zm = ring(-2, -1, zm)

    t0 = gbt_ref[0, pl.ds(0, HALF), :].astype(f32)
    for d in (2, 1, 3):
        h0[d].wait_recv()
        t0 = t0 + rh0_ref[d - 1].astype(f32)
    th0_ref[...] = t0.astype(bf16)
    p2a = [
        send(th0_ref.at[:, pl.ds(d * R, R)], p2h0_ref.at[d - 1], dev(dy=d)) for d in range(1, NY)
    ]
    gh0 = t0[:, :R]
    p2b = []
    for sl in (2, 1, 3, 0):
        t1 = gbt_ref[sl, pl.ds(HALF, HALF), pl.ds(0, R)].astype(f32)
        for d in (2, 1, 3):
            h1[sl, d].wait_recv()
            t1 = t1 + rh1_ref[d - 1, sl].astype(f32)
        if sl:
            th1_ref[sl] = t1.astype(bf16)
            p2b.append(send(th1_ref.at[sl], p2h1_ref.at[sl - 1], dev(dx=sl)))
        else:
            gh1 = t1

    def gather_loss(first, n, me, msgs):
        for copy in msgs:
            copy.wait_recv()
        t = jnp.zeros((8, R), f32)
        for i in range(n):
            t = t + lr_ref[first + lax.rem(i - me + n, n)]
        return t

    lr_ref[4] = gather_loss(0, NX, x, lmsg)
    lmsg = [send(lr_ref.at[4], lr_ref.at[4 + NY - d], dev(dy=d)) for d in range(1, NY)]

    zp = ring(1, 1, zp)
    zm = ring(-1, -1, zm)

    def unproject(grad_unit, raw_ref, inv):
        raw = raw_ref[...]
        inner = jnp.sum(raw * grad_unit, axis=1, keepdims=True)
        return (inv * grad_unit - raw * (inv * inv * inv * inner)).astype(bf16)

    for copy in p2a:
        copy.wait_recv()
    for copy in p2b:
        copy.wait_recv()
    for d in range(NX - 1):
        gh0 = gh0 + p2h0_ref[d].astype(f32)
        gh1 = gh1 + p2h1_ref[d].astype(f32)
    grad_uo = jnp.concatenate([gh0.T, gh1.T], axis=1)
    gro = unproject(grad_uo, rawo_ref, inv_o)

    q0 = chip_sum(0)
    zp.wait_recv()
    zm.wait_recv()
    grad_us = q0 + zp_ref[2].astype(f32) + zm_ref[2].astype(f32)
    grs = unproject(grad_us, raws_ref, inv_s)

    gsnd_ref[...] = jnp.where(core0, gro, grs)
    gcopy = send(gsnd_ref, grcv_ref, dev(dc=1))
    gmine_ref[...] = jnp.where(core0, grs, gro)
    gopt_ref[...] = dot_nt(gro, wo_ref[...]).astype(bf16)
    lr_ref[8] = gather_loss(4, NY, y, lmsg)
    lmsg = [send(lr_ref.at[8], lr_ref.at[8 + NZ - d], dev(dz=d)) for d in range(1, NZ)]
    gcopy.wait_recv()

    w_ref[...] = dot_nn(ft_ref[:, pl.ds(0, R)], gmine_ref[...]) + dot_nn(
        ft_ref[:, pl.ds(R, R)], grcv_ref[...])
    for ix in range(NX):
        for iy in range(NY):
            for zz in range(0, NZ, 2):
                lo = ((zz * NX + ix) * NY + iy) * 8
                hi = (((zz + 1) * NX + ix) * NY + iy) * 8
                left = jnp.concatenate(
                    [w_ref[pl.ds(lo, 8), pl.ds(0, HALF)], w_ref[pl.ds(hi, 8), pl.ds(0, HALF)]], 0)
                right = jnp.concatenate(
                    [w_ref[pl.ds(lo, 8), pl.ds(HALF, HALF)],
                     w_ref[pl.ds(hi, 8), pl.ds(HALF, HALF)]], 0)
                sx_ref[ix, pl.ds(iy * 64 + zz * 8, 16), :] = left.astype(bf16)
                sy_ref[iy, pl.ds(ix * 64 + zz * 8, 16), :] = right.astype(bf16)
    wx, wy = {}, {}
    for d in (2, 1, 3):
        wx[d] = send(sx_ref.at[lax.rem(x + d, NX)], rx_ref.at[d - 1], dev(dx=d))
        wy[d] = send(sy_ref.at[lax.rem(y + d, NY)], ry_ref.at[d - 1], dev(dy=d))
    gsar_ref[...] = dot_nt(grs, ws_ref[...]).astype(bf16)
    tx = sx_ref[x].astype(f32)
    ty = sy_ref[y].astype(f32)
    for d in (1, 3, 2):
        wx[d].wait_recv()
        tx = tx + rx_ref[d - 1].astype(f32)
        wy[d].wait_recv()
        ty = ty + ry_ref[d - 1].astype(f32)
    sx2_ref[...] = tx.astype(bf16).reshape(NY, 64, HALF)
    sy2_ref[...] = ty.astype(bf16).reshape(NX, 64, HALF)
    for d in (2, 1, 3):
        wx[d] = send(sx2_ref.at[lax.rem(y + d, NY)], rx2_ref.at[d - 1], dev(dy=d))
        wy[d] = send(sy2_ref.at[lax.rem(x + d, NX)], ry2_ref.at[d - 1], dev(dx=d))
    lr_ref[16] = gather_loss(8, NZ, z, lmsg)
    lmsg = [send(lr_ref.at[16], lr_ref.at[17], dev(dc=1))]
    tx = sx2_ref[y].astype(f32)
    ty = sy2_ref[x].astype(f32)
    for d in (1, 3, 2):
        wx[d].wait_recv()
        tx = tx + rx2_ref[d - 1].astype(f32)
        wy[d].wait_recv()
        ty = ty + ry2_ref[d - 1].astype(f32)
    u_ref[:, :, pl.ds(0, HALF)] = tx.reshape(NZ, 8, HALF)
    u_ref[:, :, pl.ds(HALF, HALF)] = ty.reshape(NZ, 8, HALF)
    wz = [
        send(u_ref.at[lax.rem(z + d, NZ)], rz_ref.at[d - 1], dev(dz=d)) for d in range(1, NZ)
    ]
    loss_ref[0] = jnp.sum(gather_loss(16, 2, c, lmsg)) * (1.0 / (2.0 * NX * NY * NZ * 2 * R))
    total = u_ref[z]
    for d in range(1, NZ):
        wz[d - 1].wait_recv()
        total = total + rz_ref[d - 1]
    fin_ref[...] = total
    last = send(fin_ref, sis_ref, dev(dc=1))
    last.wait_recv()
    other = sis_ref[...]
    s_sum = jnp.where(core0, total, other)
    o_sum = jnp.where(core0, other, total)
    gws_ref[...] = jnp.where(core0, s_sum[0:4], s_sum[4:8])
    gwo_ref[...] = jnp.where(core0, o_sum[0:4], o_sum[4:8])

    for copy in sent:
        copy.wait_send()


def local(sar_feats, opt_feats, w_sar, w_opt, logit_scale, partner):
    V = pltpu.VMEM
    scratch = [
        V((TR, E), bf16), V((E, TR), bf16), V((TC, E), bf16),
        V((NX, TR, E), f32), V((NX, TR, E), bf16), V((R, E), f32), V((R, E), f32),
        V((16, 8, R), f32), V((TR, R), f32), V((8, TC), f32),
        V((2, TR, R), f32), V((2, 8, TC), f32), V((TR, R), f32),
        V((16, 16, R), f32), V((16, 16, R), f32), V((16, 16, R), f32), V((16, 16, R), f32),
        V((16, 8, R), f32), V((8, TC), f32), V((TR, R), f32),
        V((E, E), f32), V((NX, E, E), bf16), V((3, HALF, E), bf16), V((3, NX, HALF, R), bf16),
        V((HALF, E), bf16), V((NX, HALF, R), bf16), V((3, HALF, R), bf16), V((3, HALF, R), bf16),
        V((NZ, R, E), f32), V((NZ, R, E), bf16), V((NZ, R, E), bf16), V((NZ, R, E), bf16),
        V((R, HALF), bf16), V((R, HALF), bf16), V((3, R, E), bf16), V((3, R, E), bf16),
        V((R, F), bf16), V((R, F), bf16), V((F, 2 * R), bf16),
        V((R, E), bf16), V((R, E), bf16), V((R, E), bf16), V((F, E), f32),
        V((NX, HALF, HALF), bf16), V((NY, HALF, HALF), bf16),
        V((3, HALF, HALF), bf16), V((3, HALF, HALF), bf16),
        V((NY, 64, HALF), bf16), V((NX, 64, HALF), bf16),
        V((3, 64, HALF), bf16), V((3, 64, HALF), bf16),
        V((NZ, 8, E), f32), V((NZ - 1, 8, E), f32), V((8, E), f32), V((8, E), f32),
        V((18, 8, R), f32),
        pltpu.SemaphoreType.DMA((MSGS,)), pltpu.SemaphoreType.DMA((MSGS,)),
    ]
    vm = pl.BlockSpec(memory_space=pltpu.VMEM)
    sm = pl.BlockSpec(memory_space=pltpu.SMEM)
    return pl.pallas_call(
        kernel,
        out_shape=(
            jax.ShapeDtypeStruct((1,), f32),
            jax.ShapeDtypeStruct((R, F), bf16),
            jax.ShapeDtypeStruct((R, F), bf16),
            jax.ShapeDtypeStruct((4, E), f32),
            jax.ShapeDtypeStruct((4, E), f32),
        ),
        in_specs=[vm, vm, vm, vm, sm, vm],
        out_specs=(sm, vm, vm, vm, vm),
        scratch_shapes=scratch,
        compiler_params=pltpu.CompilerParams(
            collective_id=0, has_side_effects=True, vmem_limit_bytes=62 * 1024 * 1024),
        name="contrastive",
    )(sar_feats, opt_feats, w_sar, w_opt, logit_scale, partner.reshape(NY * 2, R))


def solution(mesh):
    return jax.shard_map(
        local,
        mesh=mesh,
        in_specs=(
            P(("wide", "narrow"), None),
            P(("wide", "narrow"), None),
            P(),
            P(),
            P(),
            P("wide"),
        ),
        out_specs=(
            P(),
            P(("wide", "narrow"), None),
            P(("wide", "narrow"), None),
            P(("wide", "narrow"), None),
            P(("wide", "narrow"), None),
        ),
        check_vma=False,
    )
```

time: 1020 us -> 128 us (0.13)
  waiting for transfers between devices: 541 us -> 0 us
  blocking collectives: 385 us -> 0 us
  Pallas kernels: 0 us -> 121 us
  matrix products: 38.1 us -> 0 us
  other arithmetic: 28.8 us -> 0 us
  between operations: 17.7 us -> 3.1 us
    reduce_scatter x2 -> x0, waiting for transfers between devices: 244 us -> none  [the longest x1 227 us: local(): lax.psum_scatter(opt_terms, 'wide', scatter_dimension=0, tiled=True)]
    psum x3 -> x0, blocking collectives: 229 us -> none  [the longest x1 110 us: local(): lax.psum((jnp.sum(jnp.exp(logits - col_max[None, :]), axis=0), jnp.sum(ma...]
    unnamed x6 -> x0, waiting for transfers between devices: 189 us -> none
    pmax x2 -> x0, blocking collectives: 156 us -> none  [the longest x1 112 us: local(): col_max = lax.pmax(jnp.max(logits, axis=0), 'wide')]
    pallas_call x0 -> x1, Pallas kernels: none -> 121 us  [local(): pl.pallas_call(kernel, out_shape=(jax.ShapeDtypeStruct((1,), f32), jax.Sh...]
    all_gather x2 -> x0, waiting for transfers between devices: 109 us -> none  [the longest x1 81.8 us: local(): opt_block = lax.all_gather(unit_o, 'wide', axis=0, tiled=True)]
    dot_general x9 -> x0, matrix products: 38.1 us -> none  [the longest x1 12.8 us: local(): lax.dot_general(sar_block, opt_block, (((1,), (1,)), ((), ())), preferred...]
    reduce_sum x5 -> x0, other arithmetic: 14.8 us -> none  [the longest x1 11.4 us: local(): jnp.sum(jnp.exp(logits - col_max[None, :]), axis=0)]
  transfers between devices with their start and end apart: 5 -> 0, of which waited for: 5 -> 0; matrix products, arithmetic and copies ran while one was open for 2% -> 0% of each run, Pallas kernels for 0% -> 0%
where the time goes in v1:
time: 128 us
  Pallas kernels  121 us (95%)
  local copies, waits for them, and re-layouts  3.72 us (3%)
  between operations  3.1 us (2%)
    pallas_call x1, Pallas kernels, local(): pl.pallas_call(kernel, out_shape=(jax.ShapeDtypeStruct((1,), f32), jax.Sh...  121 us
    unnamed x10, local copies, waits for them, and re-layouts  3.72 us

profile of v1, /device:TPU:1, one launch (start us, length us, event | category | flops | bytes accessed | tf_op | source)
XLA Modules:
  0.0 127.8 jit_solution(11267334091907823457)
XLA Ops:
  1.3 120.9 %contrastive.1 = (f32[1]{0:T(128)}, bf16[128,1024]{1,0:T(8,128)(2,1)}, bf16[128,1024]{1,0:T(8,128)(2,1)}, f32[4,512]{1,0:T(4,128)}, f32[4,512]{1,0:T(4,128)}) custom-call(bf16[128,1024]{1,0:T(8,128)(2,1)} %sar_ref.1, bf16[128,1024]{1,0:T(8,128)(2,1)} %opt_ref.1, bf16[1024,512]{1,0:T(8,128)(2,1)} %ws_ref.1, bf16[1024,512]{1,0:T(8,128)(2,1)} %wo_ref.1, ...), custom_call_target="tpu_custom_call" | custom-call | tf_op jit(solution)/shard_map/contrastive/pallas_call | solution.py:518
  122.9 0.0 copy-start
  122.9 1.7 %copy.18 = bf16[128,1024]{1,0:T(8,128)(2,1)} copy(bf16[128,1024]{1,0:T(8,128)(2,1)} %get-tuple-element.11) | data formatting | bytes 524288
  124.6 0.0 copy-done
  124.6 0.0 copy-start.2
  124.6 0.7 copy.19
  125.3 0.0 copy-done.2
  125.3 0.0 copy-start.1
  125.3 0.6 copy.20
  125.9 0.1 copy-done.1
  126.0 0.6 copy.21
Async XLA Ops:
  122.9 1.7 %copy-start = (bf16[128,1024]{1,0:T(8,128)(2,1)S(1)}, bf16[128,1024]{1,0:T(8,128)(2,1)}, u32[]{:S(2)}) copy-start(bf16[128,1024]{1,0:T(8,128)(2,1)} %get-tuple-element.12) | copy-start | bytes 786436
  124.6 0.7 copy-start.2
  125.3 0.7 copy-start.1

commit v2 on v0

v2 whole, which is shorter than its diff:
```python
import jax
import jax.numpy as jnp
from jax import lax
from jax.experimental import pallas as pl
from jax.experimental.pallas import tpu as pltpu
from jax.sharding import PartitionSpec as P

NX, NY, NZ = 4, 4, 8
R = 128
E = 512
F = 1024
HALF = 256
TR = NZ * 2 * R
TC = NX * NY * R
LOG2E = 1.4426950408889634
SHIFT = 25.0
UP = 5.184705528587072e21
DOWN = 1.9287498e-22
MSGS = 256
ORDER = (0, 1, 7, 2, 6, 3, 5, 4)
NEAR = 5 * 2 * R
f32 = jnp.float32
bf16 = jnp.bfloat16
MESH = pl.DeviceIdType.MESH


def dot_nt(a, b):
    return lax.dot_general(a, b, (((1,), (1,)), ((), ())), preferred_element_type=f32)


def dot_nn(a, b):
    return jnp.dot(a, b, preferred_element_type=f32)


def kernel(
    sar_ref, opt_ref, ws_ref, wo_ref, scale_ref, partner_ref,
    loss_ref, gsar_ref, gopt_ref, gws_ref, gwo_ref,
    a_ref, at_ref, b_ref, e_ref, g_ref, raws_ref, rawo_ref,
    part_ref, prow_ref, cid_ref, racc_ref, cacc_ref, pacc_ref,
    rsnd_ref, csnd_ref, rrcv_ref, crcv_ref, lses_ref, cfac_ref, rfac_ref, rhalf_ref,
    cst_ref, rrow_ref, gbt_ref, rh0_ref, rh1_ref, th0_ref, th1_ref, p2h0_ref, p2h1_ref,
    qown_ref, qsis_ref, qrcv_ref, qsnd_ref, zp_ref, zm_ref,
    frcv_ref, ft_ref, gmine_ref, gsnd_ref, grcv_ref,
    sx_ref, sy_ref, rx_ref, ry_ref, sx2_ref, sy2_ref, rx2_ref, ry2_ref,
    u_ref, rz_ref, fin_ref, sis_ref, lr_ref,
    ssem, rsem,
):
    wide = lax.axis_index("wide")
    narrow = lax.axis_index("narrow")
    x, y, z, c = lax.rem(wide, NX), narrow // 2, wide // NX, lax.rem(narrow, 2)

    def dev(dx=0, dy=0, dz=0, dc=0):
        px = lax.rem(x + (dx % NX), NX)
        py = lax.rem(y + (dy % NY), NY)
        pz = lax.rem(z + (dz % NZ), NZ)
        pc = lax.rem(c + (dc % 2), 2)
        return (pz * NX + px, py * 2 + pc)

    plane = [(i, j) for i in range(NX) for j in range(NY) if (i, j) != (0, 0)]

    barrier = pltpu.get_barrier_semaphore()
    for i, j in plane:
        pl.semaphore_signal(barrier, inc=1, device_id=dev(dx=i, dy=j), device_id_type=MESH)
    for i in range(1, NZ):
        pl.semaphore_signal(barrier, inc=1, device_id=dev(dz=i), device_id_type=MESH)
    pl.semaphore_signal(barrier, inc=1, device_id=dev(dc=1), device_id_type=MESH)

    sent = []

    def send(src, dst, device):
        m = len(sent)
        copy = pltpu.make_async_remote_copy(
            src_ref=src, dst_ref=dst, send_sem=ssem.at[m], recv_sem=rsem.at[m],
            device_id=device, device_id_type=MESH,
        )
        copy.start()
        sent.append(copy)
        return copy

    def brow(dx, dy):
        return ((dx % NX) * NY + (dy % NY)) * R

    def arow(dz, dc):
        return (ORDER.index(dz % NZ) * 2 + dc % 2) * R

    scale = scale_ref[0]

    def project(feat_ref, w_ref, raw_ref, dst_ref):
        raw = dot_nn(feat_ref[...], w_ref[...])
        inv = lax.rsqrt(jnp.sum(raw * raw, axis=1, keepdims=True) + 1e-06)
        raw_ref[...] = raw
        dst_ref[pl.ds(0, R), :] = (raw * inv).astype(bf16)
        return inv

    inv_o = project(opt_ref, wo_ref, rawo_ref, b_ref)
    inv_s = project(sar_ref, ws_ref, raws_ref, a_ref)
    own_partner = partner_ref[pl.ds(narrow, 1), :].astype(f32)
    part_ref[0, 0] = jnp.broadcast_to(own_partner, (8, R))
    core0 = c == 0

    pl.semaphore_wait(barrier, len(plane) + NZ)

    bx, by, late, sis = {}, {}, {}, {}
    own_b = b_ref.at[pl.ds(0, R)]
    lanes = [pl.ds(0, HALF), pl.ds(HALF, HALF)]

    def zsend(h, src, dst, sign):
        return send(
            a_ref.at[pl.ds(arow(src, 0), R), lanes[h]],
            a_ref.at[pl.ds(arow(dst, 0), R), lanes[h]], dev(dz=sign))

    up = [zsend(h, 0, -1, 1) for h in range(2)]
    down = [zsend(h, 0, 1, -1) for h in range(2)]
    for d in (1, 3, 2):
        bx[d] = send(own_b, b_ref.at[pl.ds(brow(-d, 0), R)], dev(dx=d))
        by[d] = send(own_b, b_ref.at[pl.ds(brow(0, -d), R)], dev(dy=d))

    def to_sister(d):
        sis[d % NZ] = send(
            a_ref.at[pl.ds(arow(d, 0), R)], a_ref.at[pl.ds(arow(d, 1), R)], dev(dc=1))

    to_sister(0)
    parts = [
        send(part_ref.at[0, 0], part_ref.at[0, (-i) % NZ], dev(dz=i)) for i in range(1, NZ)
    ]
    sar = sar_ref[...]
    opt = opt_ref[...]
    fcopy = [
        send(sar_ref, frcv_ref.at[0], dev(dc=1)), send(opt_ref, frcv_ref.at[1], dev(dc=1))
    ]
    lane = lax.broadcasted_iota(jnp.int32, (8, R), 1)
    for i in range(NX):
        for j in range(NY):
            wx = z * NX + lax.rem(x + i, NX)
            ny = lax.rem(y + j, NY) * 2 + c
            base = (wx * (NY * 2) + ny) * R
            cid_ref[:, pl.ds(brow(i, j), R)] = (lane + base).astype(f32)

    def transpose_a(row):
        at_ref[:, pl.ds(row, R)] = a_ref[pl.ds(row, R), :].T

    def ring_step(k):
        for h in range(2):
            up[h].wait_recv()
            if k < 3 or h == 0:
                up[h] = zsend(h, -k, -k - 1, 1)
            down[h].wait_recv()
            if k < 3 or h == 1:
                down[h] = zsend(h, k, k + 1, -1)
        to_sister(-k)
        to_sister(k)

    def plane_step(d):
        bx[d].wait_recv()
        for dy in (1, 3, 2):
            late[(-d) % NX, (-dy) % NY, 0] = send(
                b_ref.at[pl.ds(brow(-d, 0), R), lanes[0]],
                b_ref.at[pl.ds(brow(-d, -dy), R), lanes[0]], dev(dy=dy))
        by[d].wait_recv()
        for dx in (1, 3, 2):
            late[(-dx) % NX, (-d) % NY, 1] = send(
                b_ref.at[pl.ds(brow(0, -d), R), lanes[1]],
                b_ref.at[pl.ds(brow(-dx, -d), R), lanes[1]], dev(dx=dx))

    ring_step(1)
    plane_step(1)
    plane_step(3)
    for k in (0, 1, -1):
        transpose_a(arow(k, 0))
    ft_ref[0, :, pl.ds(0, R)] = sar.T
    ft_ref[1, :, pl.ds(0, R)] = opt.T
    plane_step(2)
    ring_step(2)
    for k in (2, -2):
        transpose_a(arow(k, 0))
    for t in range(2):
        fcopy[t].wait_recv()
        ft_ref[t, :, pl.ds(R, R)] = frcv_ref[t].T
    for copy in parts:
        copy.wait_recv()
    pcopy = send(part_ref.at[0], part_ref.at[1], dev(dc=1))
    for k in (0, 1, -1):
        sis[k % NZ].wait_recv()
        transpose_a(arow(k, 1))
    mul = scale * (0.5 * LOG2E)
    CH = 64

    def logits(sl, lo, hi):
        for i, j, h in sorted(late):
            if i == sl and lo == 0:
                late[i, j, h].wait_recv()
        e_ref[sl, pl.ds(lo, hi - lo), :] = dot_nt(
            a_ref[pl.ds(lo, hi - lo), :], b_ref[pl.ds(sl * E, E), :])

    def exponentials(sl, lo, hi, first):
        c1 = jnp.zeros((8, E), f32)
        c2 = jnp.zeros((8, E), f32)
        for r0 in range(lo, hi, CH):
            rows = pl.ds(r0, CH)
            e = jnp.exp2(e_ref[sl, rows, :] * mul - SHIFT * LOG2E)
            e_ref[sl, rows, :] = e
            q1 = e * e
            u = e * UP
            q2 = u * u
            c1 = c1 + jnp.sum(q1.reshape(CH // 8, 8, E), axis=0)
            c2 = c2 + jnp.sum(q2.reshape(CH // 8, 8, E), axis=0)
            r1 = (q1[:, 0:128] + q1[:, 128:256]) + (q1[:, 256:384] + q1[:, 384:512])
            r2 = (q2[:, 0:128] + q2[:, 128:256]) + (q2[:, 256:384] + q2[:, 384:512])
            if not first:
                r1 = r1 + racc_ref[0, rows, :]
                r2 = r2 + racc_ref[1, rows, :]
            racc_ref[0, rows, :] = r1
            racc_ref[1, rows, :] = r2
        if lo > 0:
            c1 = c1 + cacc_ref[0, :, pl.ds(sl * E, E)]
            c2 = c2 + cacc_ref[1, :, pl.ds(sl * E, E)]
        cacc_ref[0, :, pl.ds(sl * E, E)] = c1
        cacc_ref[1, :, pl.ds(sl * E, E)] = c2

    for k in (2, -2):
        sis[k % NZ].wait_recv()
        transpose_a(arow(k, 1))
    logits(0, 0, NEAR)
    ring_step(3)
    for k in (3, -3):
        transpose_a(arow(k, 0))
    pcopy.wait_recv()
    for q in range(NZ * 2):
        prow_ref[pl.ds(q * R, R), :] = jnp.broadcast_to(
            part_ref[q % 2, ORDER[q // 2]][0:1, :], (R, R)).T

    order = (0, 1, 3, 2)
    for n, sl in enumerate(order):
        if n + 1 < NX:
            logits(order[n + 1], 0, NEAR)
        exponentials(sl, 0, NEAR, n == 0)
    for k in (3, -3):
        sis[k % NZ].wait_recv()
        transpose_a(arow(k, 1))
    up[0].wait_recv()
    down[1].wait_recv()
    to_sister(4)
    transpose_a(arow(4, 0))
    sis[4].wait_recv()
    transpose_a(arow(4, 1))
    logits(order[0], NEAR, TR)
    for n, sl in enumerate(order):
        if n + 1 < NX:
            logits(order[n + 1], NEAR, TR)
        exponentials(sl, NEAR, TR, n == 0)

    def local_lse(s1, s2):
        return jnp.where(
            s1 > DOWN, jnp.log(s1) + 2.0 * SHIFT, jnp.log(s2) - 2.0 * SHIFT)

    def combine(parts):
        top = parts[0]
        for p in parts[1:]:
            top = jnp.maximum(top, p)
        total = jnp.exp(parts[0] - top)
        for p in parts[1:]:
            total = total + jnp.exp(p - top)
        return top + jnp.log(total)

    def abs_row(q):
        return lax.rem(z + ORDER[q // 2], NZ) * 2 + lax.rem(c + q % 2, 2)

    def abs_col(p):
        return lax.rem(x + p // NY, NX) * NY + lax.rem(y + p % NY, NY)

    col = local_lse(
        jnp.sum(cacc_ref[0], axis=0, keepdims=True), jnp.sum(cacc_ref[1], axis=0, keepdims=True))
    for p in range(16):
        csnd_ref[pl.ds(abs_col(p), 1), :] = col[:, p * R : (p + 1) * R]
    cmsg = [
        send(csnd_ref, crcv_ref.at[n], dev(dx=i, dy=j)) for n, (i, j) in enumerate(plane)
    ]
    ones = jnp.ones((8, R), bf16)

    def row_sum(k):
        v = racc_ref[k]
        hi = v.astype(bf16)
        lo = (v - hi.astype(f32)).astype(bf16)
        return dot_nt(ones, hi) + dot_nt(ones, lo)

    row = local_lse(row_sum(0), row_sum(1))
    for q in range(16):
        rsnd_ref[pl.ds(abs_row(q), 1), :] = row[0:1, q * R : (q + 1) * R]
    rmsg = [send(rsnd_ref, rrcv_ref.at[d - 1], dev(dz=d)) for d in range(1, NZ)]
    for copy in cmsg:
        copy.wait_recv()
    lse_col = combine([csnd_ref[...]] + [crcv_ref[n] for n in range(len(plane))])
    root = jnp.sqrt(jnp.full((16, R), scale * 0.5, f32))
    lses_ref[0] = lse_col
    cfac_ref[...] = jnp.exp(SHIFT - 0.5 * lse_col) * root
    for p in range(16):
        cst_ref[:, pl.ds(p * R, R)] = jnp.broadcast_to(
            cfac_ref[pl.ds(abs_col(p), 1), :], (8, R))
    for copy in rmsg:
        copy.wait_recv()
    lse_row = combine([rsnd_ref[...]] + [rrcv_ref[d] for d in range(NZ - 1)])
    rhalf_ref[0] = lse_row
    rcopy = send(rhalf_ref.at[0], rhalf_ref.at[1], dev(dc=1))
    rcopy.wait_recv()
    lse_row = combine([lse_row, rhalf_ref[1]])
    lses_ref[1] = lse_row
    rfac_ref[...] = jnp.exp(SHIFT - 0.5 * lse_row) * root
    for q in range(16):
        rrow_ref[pl.ds(q * R, R), :] = jnp.broadcast_to(
            rfac_ref[pl.ds(abs_row(q), 1), :], (R, R)).T
    own_lse = lses_ref[0, pl.ds(abs_col(0), 1), :] + lses_ref[1, pl.ds(abs_row(0), 1), :]

    h0, h1, qmsg, zmsg, done = {}, {}, {}, {}, set()
    zin = {1: zp_ref, -1: zm_ref}

    def gradient(sl, d):
        d = d % NZ
        if (sl, d) in done:
            return
        done.add((sl, d))
        for r0 in range(arow(d, 0), arow(d, 0) + HALF, CH):
            rows = pl.ds(r0, CH)
            rr = rrow_ref[rows, :].reshape(CH // 8, 8, R)
            pr = prow_ref[rows, :].reshape(CH // 8, 8, R)
            pos = None
            for lg in range(NY):
                cols = pl.ds(sl * E + lg * R, R)
                e = e_ref[sl, rows, pl.ds(lg * R, R)].reshape(CH // 8, 8, R)
                u = e * rr
                v = e * cst_ref[:, cols][None]
                hit = pr == cid_ref[:, cols][None]
                g = u * u + v * v - jnp.where(hit, scale, 0.0)
                pe = jnp.where(hit, e, 0.0)
                pos = pe if pos is None else pos + pe
                g_ref[sl, rows, pl.ds(lg * R, R)] = g.reshape(CH, R).astype(bf16)
            pos = pos.reshape(CH, R)
            if sl != 2:
                pos = pos + pacc_ref[rows, :]
            pacc_ref[rows, :] = pos

    def slab(sl):
        gbt_ref[sl] = dot_nn(at_ref[...], g_ref[sl]).astype(bf16)

    def slab_send(sl):
        if sl:
            h0[sl] = send(gbt_ref.at[sl, pl.ds(0, HALF)], rh0_ref.at[sl - 1], dev(dx=sl))
        for dy in (2, 1, 3):
            h1[sl, dy] = send(
                gbt_ref.at[sl, pl.ds(HALF, HALF), pl.ds(dy * R, R)],
                rh1_ref.at[dy - 1, sl], dev(dy=dy))

    def radar(d):
        total = None
        for sl in range(NX):
            t = dot_nn(g_ref[sl, pl.ds(arow(d, 0), HALF), :], b_ref[pl.ds(sl * E, E), :])
            total = t if total is None else total + t
        qown_ref[d % NZ] = total[0:R]
        qsis_ref[d % NZ] = total[R:].astype(bf16)

    def radar_send(d):
        qmsg[d % NZ] = send(qsis_ref.at[d % NZ], qrcv_ref.at[d % NZ], dev(dc=1))

    def chip_sum(d):
        qmsg[d % NZ].wait_recv()
        return qown_ref[d % NZ] + qrcv_ref[d % NZ].astype(f32)

    def ring(k):
        q = {1: chip_sum(k), -1: chip_sum(-k)}
        for h in range(2):
            for sign in (1, -1):
                d = (sign * k) % NZ
                v = q[sign][:, h * HALF : (h + 1) * HALF]
                if k < 3 or h == (0 if sign > 0 else 1):
                    zmsg[sign, h].wait_recv()
                    v = v + zin[sign][3 - k, h].astype(f32)
                qsnd_ref[d, h] = v.astype(bf16)
                zmsg[sign, h] = send(
                    qsnd_ref.at[d, h], zin[sign].at[4 - k, h], dev(dz=sign))

    def rows_of(*ds):
        for d in ds:
            for sl in (1, 3, 0):
                gradient(sl, d)

    def col_of(sl):
        for d in range(NZ):
            gradient(sl, d)

    col_of(2)
    slab(2)
    rows_of(4)
    slab_send(2)
    radar(4)
    rows_of(3)
    radar_send(4)
    radar(3)
    rows_of(-3)
    radar_send(3)
    radar(-3)
    col_of(1)
    radar_send(-3)
    q4 = chip_sum(4).astype(bf16)
    for h, sign in ((0, 1), (1, -1)):
        qsnd_ref[4, h] = q4[:, h * HALF : (h + 1) * HALF]
        zmsg[sign, h] = send(qsnd_ref.at[4, h], zin[sign].at[0, h], dev(dz=sign))
    slab(1)
    rows_of(2, -2)
    slab_send(1)
    radar(2)
    radar(-2)
    col_of(3)
    radar_send(2)
    radar_send(-2)
    ring(3)
    slab(3)
    col_of(0)
    slab_send(3)
    slab(0)
    slab_send(0)
    radar(1)
    radar(-1)
    radar_send(1)
    radar_send(-1)
    radar(0)
    radar_send(0)
    ring(2)

    pos = pacc_ref[...]
    pos = jnp.where(pos > 0.0, 2.0 * (jnp.log(jnp.where(pos > 0.0, pos, 1.0)) + SHIFT), 0.0)
    pos = jnp.sum(pos.reshape(TR // 8, 8, R), axis=0)
    row0 = lax.broadcasted_iota(jnp.int32, (8, R), 0) == 0
    both = jnp.broadcast_to(own_lse, (8, R))
    lr_ref[0] = jnp.where(row0, both, 0.0) - 2.0 * pos
    lmsg = [send(lr_ref.at[0], lr_ref.at[NX - d], dev(dx=d)) for d in range(1, NX)]

    def gather_loss(first, n, me, msgs):
        for copy in msgs:
            copy.wait_recv()
        t = jnp.zeros((8, R), f32)
        for i in range(n):
            t = t + lr_ref[first + lax.rem(i - me + n, n)]
        return t

    ring(1)

    t0 = gbt_ref[0, pl.ds(0, HALF), :].astype(f32)
    for d in (2, 1, 3):
        h0[d].wait_recv()
        t0 = t0 + rh0_ref[d - 1].astype(f32)
    th0_ref[...] = t0.astype(bf16)
    p2a = [
        send(th0_ref.at[:, pl.ds(d * R, R)], p2h0_ref.at[d - 1], dev(dy=d)) for d in range(1, NY)
    ]
    gh0 = t0[:, :R]
    p2b = []
    for sl in (2, 1, 3, 0):
        t1 = gbt_ref[sl, pl.ds(HALF, HALF), pl.ds(0, R)].astype(f32)
        for d in (2, 1, 3):
            h1[sl, d].wait_recv()
            t1 = t1 + rh1_ref[d - 1, sl].astype(f32)
        if sl:
            th1_ref[sl] = t1.astype(bf16)
            p2b.append(send(th1_ref.at[sl], p2h1_ref.at[sl - 1], dev(dx=sl)))
        else:
            gh1 = t1

    def unproject(grad_unit, raw_ref, inv):
        raw = raw_ref[...]
        inner = jnp.sum(raw * grad_unit, axis=1, keepdims=True)
        return (inv * grad_unit - raw * (inv * inv * inv * inner)).astype(bf16)

    def head_exchange(t, grad):
        gsnd_ref[t] = jnp.where(core0, grad[:, HALF:], grad[:, :HALF])
        gmine_ref[t] = jnp.where(core0, grad[:, :HALF], grad[:, HALF:])
        return send(gsnd_ref.at[t], grcv_ref.at[t], dev(dc=1))

    def head_first(t, copy):
        copy.wait_recv()
        w = dot_nn(ft_ref[t, :, pl.ds(0, R)], gmine_ref[t]) + dot_nn(
            ft_ref[t, :, pl.ds(R, R)], grcv_ref[t])
        w = w.reshape(NZ, NX, NY, 8, HALF)
        for ix in range(NX):
            for iy in range(NY):
                v = w[:, ix, iy].reshape(NZ * 8, HALF).astype(bf16)
                sx_ref[t, ix, pl.ds(iy * 64, 64), :] = v[:, :R]
                sy_ref[t, iy, pl.ds(ix * 64, 64), :] = v[:, R:]
        out = []
        for d in (2, 1, 3):
            out.append(send(sx_ref.at[t, lax.rem(x + d, NX)], rx_ref.at[t, d - 1], dev(dx=d)))
            out.append(send(sy_ref.at[t, lax.rem(y + d, NY)], ry_ref.at[t, d - 1], dev(dy=d)))
        return out

    def head_second(t, msgs):
        tx = sx_ref[t, x].astype(f32)
        ty = sy_ref[t, y].astype(f32)
        for copy in msgs:
            copy.wait_recv()
        for d in range(3):
            tx = tx + rx_ref[t, d].astype(f32)
            ty = ty + ry_ref[t, d].astype(f32)
        sx2_ref[t] = tx.astype(bf16).reshape(NY, 64, R)
        sy2_ref[t] = ty.astype(bf16).reshape(NX, 64, R)
        out = []
        for d in (2, 1, 3):
            out.append(send(sx2_ref.at[t, lax.rem(y + d, NY)], rx2_ref.at[t, d - 1], dev(dy=d)))
            out.append(send(sy2_ref.at[t, lax.rem(x + d, NX)], ry2_ref.at[t, d - 1], dev(dx=d)))
        return out

    def head_third(t, msgs):
        tx = sx2_ref[t, y].astype(f32)
        ty = sy2_ref[t, x].astype(f32)
        for copy in msgs:
            copy.wait_recv()
        for d in range(3):
            tx = tx + rx2_ref[t, d].astype(f32)
            ty = ty + ry2_ref[t, d].astype(f32)
        u_ref[t, :, :, pl.ds(0, R)] = tx.reshape(NZ, 8, R)
        u_ref[t, :, :, pl.ds(R, R)] = ty.reshape(NZ, 8, R)
        return [
            send(u_ref.at[t, lax.rem(z + d, NZ)], rz_ref.at[t, d - 1], dev(dz=d))
            for d in (4, 3, 5, 2, 6, 1, 7)
        ]

    def head_fourth(t, msgs):
        total = u_ref[t, z]
        for copy in msgs:
            copy.wait_recv()
        for d in range(NZ - 1):
            total = total + rz_ref[t, d]
        fin_ref[t] = total
        return send(fin_ref.at[t], sis_ref.at[t], dev(dc=1))

    def head_out(t, copy, out_ref):
        copy.wait_recv()
        own = fin_ref[t]
        other = sis_ref[t]
        out_ref[:, pl.ds(0, HALF)] = jnp.where(core0, own[0:4], other[4:8])
        out_ref[:, pl.ds(HALF, HALF)] = jnp.where(core0, other[0:4], own[4:8])

    q0 = chip_sum(0)
    halves = []
    for h in range(2):
        zmsg[1, h].wait_recv()
        zmsg[-1, h].wait_recv()
        halves.append(
            q0[:, h * HALF : (h + 1) * HALF]
            + (zp_ref[3, h].astype(f32) + zm_ref[3, h].astype(f32)))
    grs = unproject(jnp.concatenate(halves, axis=1), raws_ref, inv_s)
    smsg = head_exchange(0, grs)
    lr_ref[4] = gather_loss(0, NX, x, lmsg)
    lmsg = [send(lr_ref.at[4], lr_ref.at[4 + NY - d], dev(dy=d)) for d in range(1, NY)]
    smsg = head_first(0, smsg)

    for copy in p2a + p2b:
        copy.wait_recv()
    for d in range(NX - 1):
        gh0 = gh0 + p2h0_ref[d].astype(f32)
        gh1 = gh1 + p2h1_ref[d].astype(f32)
    gro = unproject(jnp.concatenate([gh0.T, gh1.T], axis=1), rawo_ref, inv_o)
    omsg = head_exchange(1, gro)
    gsar_ref[...] = dot_nt(grs, ws_ref[...]).astype(bf16)
    omsg = head_first(1, omsg)
    gopt_ref[...] = dot_nt(gro, wo_ref[...]).astype(bf16)
    lr_ref[8] = gather_loss(4, NY, y, lmsg)
    lmsg = [send(lr_ref.at[8], lr_ref.at[8 + NZ - d], dev(dz=d)) for d in range(1, NZ)]
    smsg = head_second(0, smsg)
    omsg = head_second(1, omsg)
    lr_ref[16] = gather_loss(8, NZ, z, lmsg)
    lmsg = [send(lr_ref.at[16], lr_ref.at[17], dev(dc=1))]
    smsg = head_third(0, smsg)
    omsg = head_third(1, omsg)
    loss_ref[0] = jnp.sum(gather_loss(16, 2, c, lmsg)) * (1.0 / (2.0 * NX * NY * NZ * 2 * R))
    smsg = head_fourth(0, smsg)
    omsg = head_fourth(1, omsg)
    head_out(0, smsg, gws_ref)
    head_out(1, omsg, gwo_ref)

    for copy in sent:
        copy.wait_send()


def local(sar_feats, opt_feats, w_sar, w_opt, logit_scale, partner):
    V = pltpu.VMEM
    scratch = [
        V((TR, E), bf16), V((E, TR), bf16), V((TC, E), bf16),
        V((NX, TR, E), f32), V((NX, TR, E), bf16), V((R, E), f32), V((R, E), f32),
        V((2, NZ, 8, R), f32), V((TR, R), f32), V((8, TC), f32),
        V((2, TR, R), f32), V((2, 8, TC), f32), V((TR, R), f32),
        V((16, R), f32), V((16, R), f32), V((NZ - 1, 16, R), f32), V((15, 16, R), f32),
        V((2, 16, R), f32), V((16, R), f32), V((16, R), f32), V((2, 16, R), f32),
        V((8, TC), f32), V((TR, R), f32), V((NX, E, E), bf16), V((3, HALF, E), bf16), V((3, NX, HALF, R), bf16),
        V((HALF, E), bf16), V((NX, HALF, R), bf16), V((3, HALF, R), bf16), V((3, HALF, R), bf16),
        V((NZ, R, E), f32), V((NZ, R, E), bf16), V((NZ, R, E), bf16), V((NZ, 2, R, HALF), bf16),
        V((4, 2, R, HALF), bf16), V((4, 2, R, HALF), bf16),
        V((2, R, F), bf16), V((2, F, 2 * R), bf16),
        V((2, R, HALF), bf16), V((2, R, HALF), bf16), V((2, R, HALF), bf16),
        V((2, NX, HALF, R), bf16), V((2, NY, HALF, R), bf16),
        V((2, 3, HALF, R), bf16), V((2, 3, HALF, R), bf16),
        V((2, NY, 64, R), bf16), V((2, NX, 64, R), bf16),
        V((2, 3, 64, R), bf16), V((2, 3, 64, R), bf16),
        V((2, NZ, 8, HALF), f32), V((2, NZ - 1, 8, HALF), f32),
        V((2, 8, HALF), f32), V((2, 8, HALF), f32),
        V((18, 8, R), f32),
        pltpu.SemaphoreType.DMA((MSGS,)), pltpu.SemaphoreType.DMA((MSGS,)),
    ]
    vm = pl.BlockSpec(memory_space=pltpu.VMEM)
    sm = pl.BlockSpec(memory_space=pltpu.SMEM)
    shapes = (
        jax.ShapeDtypeStruct((1,), f32),
        jax.ShapeDtypeStruct((R, F), bf16),
        jax.ShapeDtypeStruct((R, F), bf16),
        jax.ShapeDtypeStruct((4, E), f32),
        jax.ShapeDtypeStruct((4, E), f32),
    )
    outs = pl.pallas_call(
        kernel,
        out_shape=shapes,
        in_specs=[vm, vm, vm, vm, sm, vm],
        out_specs=(sm, vm, vm, vm, vm),
        scratch_shapes=scratch,
        compiler_params=pltpu.CompilerParams(
            collective_id=0, has_side_effects=True, vmem_limit_bytes=62 * 1024 * 1024),
        name="contrastive",
    )(sar_feats, opt_feats, w_sar, w_opt, logit_scale, partner.reshape(NY * 2, R))
    return pl.pallas_call(
        hand_over,
        out_shape=shapes,
        in_specs=[sm, vm, vm, vm, vm],
        out_specs=(sm, vm, vm, vm, vm),
        name="hand_over",
    )(*outs)


def hand_over(l_in, a_in, b_in, c_in, d_in, l_out, a_out, b_out, c_out, d_out):
    l_out[0] = l_in[0]
    for i, o in ((a_in, a_out), (b_in, b_out), (c_in, c_out), (d_in, d_out)):
        o[...] = i[...]


def solution(mesh):
    return jax.shard_map(
        local,
        mesh=mesh,
        in_specs=(
            P(("wide", "narrow"), None),
            P(("wide", "narrow"), None),
            P(),
            P(),
            P(),
            P("wide"),
        ),
        out_specs=(
            P(),
            P(("wide", "narrow"), None),
            P(("wide", "narrow"), None),
            P(("wide", "narrow"), None),
            P(("wide", "narrow"), None),
        ),
        check_vma=False,
    )
```

time: 1020 us -> 96.9 us (0.10)
  waiting for transfers between devices: 541 us -> 0 us
  blocking collectives: 385 us -> 0 us
  Pallas kernels: 0 us -> 95.3 us
  matrix products: 38.1 us -> 0 us
  other arithmetic: 28.8 us -> 0 us
  between operations: 17.7 us -> 1.47 us
    reduce_scatter x2 -> x0, waiting for transfers between devices: 244 us -> none  [the longest x1 227 us: local(): lax.psum_scatter(opt_terms, 'wide', scatter_dimension=0, tiled=True)]
    psum x3 -> x0, blocking collectives: 229 us -> none  [the longest x1 110 us: local(): lax.psum((jnp.sum(jnp.exp(logits - col_max[None, :]), axis=0), jnp.sum(ma...]
    unnamed x6 -> x0, waiting for transfers between devices: 189 us -> none
    pmax x2 -> x0, blocking collectives: 156 us -> none  [the longest x1 112 us: local(): col_max = lax.pmax(jnp.max(logits, axis=0), 'wide')]
    all_gather x2 -> x0, waiting for transfers between devices: 109 us -> none  [the longest x1 81.8 us: local(): opt_block = lax.all_gather(unit_o, 'wide', axis=0, tiled=True)]
    pallas_call x0 -> x2, Pallas kernels: none -> 95.3 us  [the longest x1 92.8 us: local(): pl.pallas_call(kernel, out_shape=shapes, in_specs=[vm, vm, vm, vm, sm, vm...]
    dot_general x9 -> x0, matrix products: 38.1 us -> none  [the longest x1 12.8 us: local(): lax.dot_general(sar_block, opt_block, (((1,), (1,)), ((), ())), preferred...]
    reduce_sum x5 -> x0, other arithmetic: 14.8 us -> none  [the longest x1 11.4 us: local(): jnp.sum(jnp.exp(logits - col_max[None, :]), axis=0)]
  transfers between devices with their start and end apart: 5 -> 0, of which waited for: 5 -> 0; matrix products, arithmetic and copies ran while one was open for 2% -> 0% of each run, Pallas kernels for 0% -> 0%
where the time goes in v2:
time: 96.9 us; the launch traced here: 96.7 us
  Pallas kernels  95.3 us (98%)
  between operations  1.47 us (2%)
    pallas_call x1, Pallas kernels, local(): pl.pallas_call(kernel, out_shape=shapes, in_specs=[vm, vm, vm, vm, sm, vm...  92.8 us
    pallas_call x1, Pallas kernels, local(): pl.pallas_call(hand_over, out_shape=shapes, in_specs=[sm, vm, vm, vm, vm]...  2.46 us

profile of v2, /device:TPU:1, one launch (start us, length us, event | category | flops | bytes accessed | tf_op | source)
XLA Modules:
  0.0 96.7 jit_solution(5675572731814888389)
XLA Ops:
  1.3 92.8 %contrastive.1 = (f32[1]{0:T(128)}, bf16[128,1024]{1,0:T(8,128)(2,1)}, bf16[128,1024]{1,0:T(8,128)(2,1)}, f32[4,512]{1,0:T(4,128)}, f32[4,512]{1,0:T(4,128)}) custom-call(bf16[128,1024]{1,0:T(8,128)(2,1)} %sar_ref.1, bf16[128,1024]{1,0:T(8,128)(2,1)} %opt_ref.1, bf16[1024,512]{1,0:T(8,128)(2,1)} %ws_ref.1, bf16[1024,512]{1,0:T(8,128)(2,1)} %wo_ref.1, ...), custom_call_target="tpu_custom_call" | custom-call | tf_op jit(solution)/shard_map/contrastive/pallas_call | solution.py:615
  94.1 2.5 %hand_over.1 = (f32[1]{0:T(128)}, bf16[128,1024]{1,0:T(8,128)(2,1)}, bf16[128,1024]{1,0:T(8,128)(2,1)}, f32[4,512]{1,0:T(4,128)}, f32[4,512]{1,0:T(4,128)}) custom-call(f32[1]{0:T(128)} %get-tuple-element.10.l_in, bf16[128,1024]{1,0:T(8,128)(2,1)} %get-tuple-element.11.a_in, bf16[128,1024]{1,0:T(8,128)(2,1)} %get-tuple-element.12.b_in, ...), custom_call_target="tpu_custom_call" | custom-call | tf_op jit(solution)/shard_map/hand_over/pallas_call | solution.py:625

commit v3 on v2

--- a/solution.py
+++ b/solution.py
@@ -33,7 +33,7 @@
 
 
 def kernel(
-    sar_ref, opt_ref, ws_ref, wo_ref, scale_ref, partner_ref,
+    sar_in, opt_in, ws_in, wo_in, scale_ref, partner_ref,
     loss_ref, gsar_ref, gopt_ref, gws_ref, gwo_ref,
     a_ref, at_ref, b_ref, e_ref, g_ref, raws_ref, rawo_ref,
     part_ref, prow_ref, cid_ref, racc_ref, cacc_ref, pacc_ref,
@@ -43,7 +43,7 @@
     frcv_ref, ft_ref, gmine_ref, gsnd_ref, grcv_ref,
     sx_ref, sy_ref, rx_ref, ry_ref, sx2_ref, sy2_ref, rx2_ref, ry2_ref,
     u_ref, rz_ref, fin_ref, sis_ref, lr_ref,
-    ssem, rsem,
+    sar_ref, opt_ref, ws_ref, wo_ref, ssem, rsem, lsem,
 ):
     wide = lax.axis_index("wide")
     narrow = lax.axis_index("narrow")
@@ -65,7 +65,28 @@
         pl.semaphore_signal(barrier, inc=1, device_id=dev(dz=i), device_id_type=MESH)
     pl.semaphore_signal(barrier, inc=1, device_id=dev(dc=1), device_id_type=MESH)
 
+    loads = []
+    for n, (src, dst) in enumerate(
+        ((opt_in, opt_ref), (wo_in, wo_ref), (sar_in, sar_ref), (ws_in, ws_ref))
+    ):
+        copy = pltpu.make_async_copy(src, dst, lsem.at[n])
+        copy.start()
+        loads.append(copy)
+
     sent = []
+    settled = []
+    early = []
+
+    def sent_off(copy):
+        copy.wait_send()
+        early.append(copy)
+
+    def settle(upto):
+        while len(settled) < upto:
+            copy = sent[len(settled)]
+            if not any(copy is e for e in early):
+                copy.wait_send()
+            settled.append(True)
 
     def send(src, dst, device):
         m = len(sent)
@@ -92,7 +113,11 @@
         dst_ref[pl.ds(0, R), :] = (raw * inv).astype(bf16)
         return inv
 
+    loads[0].wait()
+    loads[1].wait()
     inv_o = project(opt_ref, wo_ref, rawo_ref, b_ref)
+    loads[2].wait()
+    loads[3].wait()
     inv_s = project(sar_ref, ws_ref, raws_ref, a_ref)
     own_partner = partner_ref[pl.ds(narrow, 1), :].astype(f32)
     part_ref[0, 0] = jnp.broadcast_to(own_partner, (8, R))
@@ -185,19 +210,18 @@
     mul = scale * (0.5 * LOG2E)
     CH = 64
 
-    def logits(sl, lo, hi):
+    def logits(sl, lo):
         for i, j, h in sorted(late):
             if i == sl and lo == 0:
                 late[i, j, h].wait_recv()
-        e_ref[sl, pl.ds(lo, hi - lo), :] = dot_nt(
-            a_ref[pl.ds(lo, hi - lo), :], b_ref[pl.ds(sl * E, E), :])
-
-    def exponentials(sl, lo, hi, first):
+        return dot_nt(a_ref[pl.ds(lo, HALF), :], b_ref[pl.ds(sl * E, E), :])
+
+    def exponentials(sl, lo, value):
         c1 = jnp.zeros((8, E), f32)
         c2 = jnp.zeros((8, E), f32)
-        for r0 in range(lo, hi, CH):
-            rows = pl.ds(r0, CH)
-            e = jnp.exp2(e_ref[sl, rows, :] * mul - SHIFT * LOG2E)
+        for r0 in range(0, HALF, CH):
+            rows = pl.ds(lo + r0, CH)
+            e = jnp.exp2(value[r0 : r0 + CH] * mul - SHIFT * LOG2E)
             e_ref[sl, rows, :] = e
             q1 = e * e
             u = e * UP
@@ -206,7 +230,7 @@
             c2 = c2 + jnp.sum(q2.reshape(CH // 8, 8, E), axis=0)
             r1 = (q1[:, 0:128] + q1[:, 128:256]) + (q1[:, 256:384] + q1[:, 384:512])
             r2 = (q2[:, 0:128] + q2[:, 128:256]) + (q2[:, 256:384] + q2[:, 384:512])
-            if not first:
+            if sl > 0:
                 r1 = r1 + racc_ref[0, rows, :]
                 r2 = r2 + racc_ref[1, rows, :]
             racc_ref[0, rows, :] = r1
@@ -217,10 +241,18 @@
         cacc_ref[0, :, pl.ds(sl * E, E)] = c1
         cacc_ref[1, :, pl.ds(sl * E, E)] = c2
 
+    def tiles(lo, hi, *slabs):
+        todo = [(sl, r0) for sl in slabs for r0 in range(lo, hi, HALF)]
+        value = logits(*todo[0])
+        for n, tile in enumerate(todo):
+            ahead = logits(*todo[n + 1]) if n + 1 < len(todo) else None
+            exponentials(*tile, value)
+            value = ahead
+
     for k in (2, -2):
         sis[k % NZ].wait_recv()
         transpose_a(arow(k, 1))
-    logits(0, 0, NEAR)
+    tiles(0, 3 * HALF, 0)
     ring_step(3)
     for k in (3, -3):
         transpose_a(arow(k, 0))
@@ -229,29 +261,33 @@
         prow_ref[pl.ds(q * R, R), :] = jnp.broadcast_to(
             part_ref[q % 2, ORDER[q // 2]][0:1, :], (R, R)).T
 
-    order = (0, 1, 3, 2)
-    for n, sl in enumerate(order):
-        if n + 1 < NX:
-            logits(order[n + 1], 0, NEAR)
-        exponentials(sl, 0, NEAR, n == 0)
-    for k in (3, -3):
-        sis[k % NZ].wait_recv()
-        transpose_a(arow(k, 1))
+    def local_lse(s1, s2):
+        return jnp.where(
+            s1 > DOWN, jnp.log(s1) + 2.0 * SHIFT, jnp.log(s2) - 2.0 * SHIFT)
+
+    ones = jnp.ones((8, R), bf16)
+
+    def row_sum(k, lo, hi):
+        v = racc_ref[k, pl.ds(lo, hi - lo), :]
+        top = v.astype(bf16)
+        rest = (v - top.astype(f32)).astype(bf16)
+        return dot_nt(ones, top) + dot_nt(ones, rest)
+
+    tiles(3 * HALF, NEAR, 0)
+    tiles(0, NEAR, 1)
     up[0].wait_recv()
     down[1].wait_recv()
     to_sister(4)
     transpose_a(arow(4, 0))
+    for k in (3, -3):
+        sis[k % NZ].wait_recv()
+        transpose_a(arow(k, 1))
+    tiles(0, NEAR, 3, 2)
+    near_row = local_lse(row_sum(0, 0, NEAR), row_sum(1, 0, NEAR))
     sis[4].wait_recv()
     transpose_a(arow(4, 1))
-    logits(order[0], NEAR, TR)
-    for n, sl in enumerate(order):
-        if n + 1 < NX:
-            logits(order[n + 1], NEAR, TR)
-        exponentials(sl, NEAR, TR, n == 0)
-
-    def local_lse(s1, s2):
-        return jnp.where(
-            s1 > DOWN, jnp.log(s1) + 2.0 * SHIFT, jnp.log(s2) - 2.0 * SHIFT)
+    gathered = len(sent)
+    tiles(NEAR, TR, 0, 1, 3, 2)
 
     def combine(parts):
         top = parts[0]
@@ -268,6 +304,12 @@
     def abs_col(p):
         return lax.rem(x + p // NY, NX) * NY + lax.rem(y + p % NY, NY)
 
+    far_row = local_lse(row_sum(0, NEAR, TR), row_sum(1, NEAR, TR))
+    for q in range(16):
+        v = near_row[0:1, q * R : (q + 1) * R] if q < 10 else far_row[
+            0:1, (q - 10) * R : (q - 9) * R]
+        rsnd_ref[pl.ds(abs_row(q), 1), :] = v
+    rmsg = [send(rsnd_ref, rrcv_ref.at[d - 1], dev(dz=d)) for d in range(1, NZ)]
     col = local_lse(
         jnp.sum(cacc_ref[0], axis=0, keepdims=True), jnp.sum(cacc_ref[1], axis=0, keepdims=True))
     for p in range(16):
@@ -275,18 +317,7 @@
     cmsg = [
         send(csnd_ref, crcv_ref.at[n], dev(dx=i, dy=j)) for n, (i, j) in enumerate(plane)
     ]
-    ones = jnp.ones((8, R), bf16)
-
-    def row_sum(k):
-        v = racc_ref[k]
-        hi = v.astype(bf16)
-        lo = (v - hi.astype(f32)).astype(bf16)
-        return dot_nt(ones, hi) + dot_nt(ones, lo)
-
-    row = local_lse(row_sum(0), row_sum(1))
-    for q in range(16):
-        rsnd_ref[pl.ds(abs_row(q), 1), :] = row[0:1, q * R : (q + 1) * R]
-    rmsg = [send(rsnd_ref, rrcv_ref.at[d - 1], dev(dz=d)) for d in range(1, NZ)]
+    settle(gathered)
     for copy in cmsg:
         copy.wait_recv()
     lse_col = combine([csnd_ref[...]] + [crcv_ref[n] for n in range(len(plane))])
@@ -332,14 +363,14 @@
                 g = u * u + v * v - jnp.where(hit, scale, 0.0)
                 pe = jnp.where(hit, e, 0.0)
                 pos = pe if pos is None else pos + pe
-                g_ref[sl, rows, pl.ds(lg * R, R)] = g.reshape(CH, R).astype(bf16)
+                g_ref[rows, cols] = g.reshape(CH, R).astype(bf16)
             pos = pos.reshape(CH, R)
             if sl != 2:
                 pos = pos + pacc_ref[rows, :]
             pacc_ref[rows, :] = pos
 
     def slab(sl):
-        gbt_ref[sl] = dot_nn(at_ref[...], g_ref[sl]).astype(bf16)
+        gbt_ref[sl] = dot_nn(at_ref[...], g_ref[:, pl.ds(sl * E, E)]).astype(bf16)
 
     def slab_send(sl):
         if sl:
@@ -349,13 +380,12 @@
                 gbt_ref.at[sl, pl.ds(HALF, HALF), pl.ds(dy * R, R)],
                 rh1_ref.at[dy - 1, sl], dev(dy=dy))
 
-    def radar(d):
-        total = None
-        for sl in range(NX):
-            t = dot_nn(g_ref[sl, pl.ds(arow(d, 0), HALF), :], b_ref[pl.ds(sl * E, E), :])
-            total = t if total is None else total + t
-        qown_ref[d % NZ] = total[0:R]
-        qsis_ref[d % NZ] = total[R:].astype(bf16)
+    def radar(*ds):
+        rows = pl.ds(arow(ds[0], 0), len(ds) * HALF)
+        total = dot_nn(g_ref[rows, :], b_ref[...])
+        for n, d in enumerate(ds):
+            qown_ref[d % NZ] = total[n * HALF : n * HALF + R]
+            qsis_ref[d % NZ] = total[n * HALF + R : (n + 1) * HALF].astype(bf16)
 
     def radar_send(d):
         qmsg[d % NZ] = send(qsis_ref.at[d % NZ], qrcv_ref.at[d % NZ], dev(dc=1))
@@ -364,18 +394,20 @@
         qmsg[d % NZ].wait_recv()
         return qown_ref[d % NZ] + qrcv_ref[d % NZ].astype(f32)
 
-    def ring(k):
-        q = {1: chip_sum(k), -1: chip_sum(-k)}
-        for h in range(2):
-            for sign in (1, -1):
-                d = (sign * k) % NZ
-                v = q[sign][:, h * HALF : (h + 1) * HALF]
-                if k < 3 or h == (0 if sign > 0 else 1):
-                    zmsg[sign, h].wait_recv()
-                    v = v + zin[sign][3 - k, h].astype(f32)
-                qsnd_ref[d, h] = v.astype(bf16)
-                zmsg[sign, h] = send(
-                    qsnd_ref.at[d, h], zin[sign].at[4 - k, h], dev(dz=sign))
+    def ring(k, chain):
+        for sign in (1, -1):
+            h = chain if sign > 0 else 1 - chain
+            d = (sign * k) % NZ
+            v = qown_ref[d, :, lanes[h]] + qrcv_ref[d, :, lanes[h]].astype(f32)
+            if k < 3 or (k == 3 and chain == 0):
+                zmsg[sign, h].wait_recv()
+                v = v + zin[sign][3 - k, h].astype(f32)
+            qsnd_ref[d, h] = v.astype(bf16)
+            zmsg[sign, h] = send(qsnd_ref.at[d, h], zin[sign].at[4 - k, h], dev(dz=sign))
+
+    def arrived(*ds):
+        for d in ds:
+            qmsg[d % NZ].wait_recv()
 
     def rows_of(*ds):
         for d in ds:
@@ -386,44 +418,48 @@
         for d in range(NZ):
             gradient(sl, d)
 
+    stats = len(sent)
     col_of(2)
     slab(2)
     rows_of(4)
     slab_send(2)
     radar(4)
-    rows_of(3)
+    rows_of(3, -3)
     radar_send(4)
-    radar(3)
-    rows_of(-3)
+    radar(3, -3)
+    col_of(1)
     radar_send(3)
-    radar(-3)
-    col_of(1)
     radar_send(-3)
-    q4 = chip_sum(4).astype(bf16)
-    for h, sign in ((0, 1), (1, -1)):
-        qsnd_ref[4, h] = q4[:, h * HALF : (h + 1) * HALF]
-        zmsg[sign, h] = send(qsnd_ref.at[4, h], zin[sign].at[0, h], dev(dz=sign))
+    arrived(4)
+    ring(4, 0)
     slab(1)
     rows_of(2, -2)
+    arrived(3, -3)
+    ring(3, 1)
     slab_send(1)
-    radar(2)
-    radar(-2)
+    radar(2, -2)
     col_of(3)
     radar_send(2)
     radar_send(-2)
-    ring(3)
+    ring(3, 0)
     slab(3)
     col_of(0)
     slab_send(3)
+    arrived(2, -2)
+    ring(2, 1)
     slab(0)
     slab_send(0)
-    radar(1)
-    radar(-1)
+    ring(2, 0)
+    radar(1, -1)
     radar_send(1)
     radar_send(-1)
     radar(0)
     radar_send(0)
-    ring(2)
+    arrived(1, -1)
+    ring(1, 1)
+    ring(1, 0)
+    reduced = len(sent)
+    settle(stats)
 
     pos = pacc_ref[...]
     pos = jnp.where(pos > 0.0, 2.0 * (jnp.log(jnp.where(pos > 0.0, pos, 1.0)) + SHIFT), 0.0)
@@ -441,7 +477,6 @@
             t = t + lr_ref[first + lax.rem(i - me + n, n)]
         return t
 
-    ring(1)
 
     t0 = gbt_ref[0, pl.ds(0, HALF), :].astype(f32)
     for d in (2, 1, 3):
@@ -537,6 +572,7 @@
         out_ref[:, pl.ds(0, HALF)] = jnp.where(core0, own[0:4], other[4:8])
         out_ref[:, pl.ds(HALF, HALF)] = jnp.where(core0, other[0:4], own[4:8])
 
+    settle(reduced)
     q0 = chip_sum(0)
     halves = []
     for h in range(2):
@@ -558,11 +594,12 @@
         gh1 = gh1 + p2h1_ref[d].astype(f32)
     gro = unproject(jnp.concatenate([gh0.T, gh1.T], axis=1), rawo_ref, inv_o)
     omsg = head_exchange(1, gro)
+    omsg = head_first(1, omsg)
     gsar_ref[...] = dot_nt(grs, ws_ref[...]).astype(bf16)
-    omsg = head_first(1, omsg)
     gopt_ref[...] = dot_nt(gro, wo_ref[...]).astype(bf16)
     lr_ref[8] = gather_loss(4, NY, y, lmsg)
     lmsg = [send(lr_ref.at[8], lr_ref.at[8 + NZ - d], dev(dz=d)) for d in range(1, NZ)]
+    heads = len(sent)
     smsg = head_second(0, smsg)
     omsg = head_second(1, omsg)
     lr_ref[16] = gather_loss(8, NZ, z, lmsg)
@@ -570,20 +607,20 @@
     smsg = head_third(0, smsg)
     omsg = head_third(1, omsg)
     loss_ref[0] = jnp.sum(gather_loss(16, 2, c, lmsg)) * (1.0 / (2.0 * NX * NY * NZ * 2 * R))
+    settle(heads)
     smsg = head_fourth(0, smsg)
     omsg = head_fourth(1, omsg)
     head_out(0, smsg, gws_ref)
     head_out(1, omsg, gwo_ref)
 
-    for copy in sent:
-        copy.wait_send()
+    settle(len(sent))
 
 
 def local(sar_feats, opt_feats, w_sar, w_opt, logit_scale, partner):
     V = pltpu.VMEM
     scratch = [
         V((TR, E), bf16), V((E, TR), bf16), V((TC, E), bf16),
-        V((NX, TR, E), f32), V((NX, TR, E), bf16), V((R, E), f32), V((R, E), f32),
+        V((NX, TR, E), f32), V((TR, TC), bf16), V((R, E), f32), V((R, E), f32),
         V((2, NZ, 8, R), f32), V((TR, R), f32), V((8, TC), f32),
         V((2, TR, R), f32), V((2, 8, TC), f32), V((TR, R), f32),
         V((16, R), f32), V((16, R), f32), V((NZ - 1, 16, R), f32), V((15, 16, R), f32),
@@ -601,9 +638,12 @@
         V((2, NZ, 8, HALF), f32), V((2, NZ - 1, 8, HALF), f32),
         V((2, 8, HALF), f32), V((2, 8, HALF), f32),
         V((18, 8, R), f32),
+        V((R, F), bf16), V((R, F), bf16), V((F, E), bf16), V((F, E), bf16),
         pltpu.SemaphoreType.DMA((MSGS,)), pltpu.SemaphoreType.DMA((MSGS,)),
+        pltpu.SemaphoreType.DMA((4,)),
     ]
     vm = pl.BlockSpec(memory_space=pltpu.VMEM)
+    hb = pl.BlockSpec(memory_space=pl.ANY)
     sm = pl.BlockSpec(memory_space=pltpu.SMEM)
     shapes = (
         jax.ShapeDtypeStruct((1,), f32),
@@ -615,7 +655,7 @@
     outs = pl.pallas_call(
         kernel,
         out_shape=shapes,
-        in_specs=[vm, vm, vm, vm, sm, vm],
+        in_specs=[hb, hb, hb, hb, sm, vm],
         out_specs=(sm, vm, vm, vm, vm),
         scratch_shapes=scratch,
         compiler_params=pltpu.CompilerParams(

time: 96.9 us -> 93.5 us (0.965)
  Pallas kernels: 95.3 us -> 91.9 us
    pallas_call x1, Pallas kernels: 92.8 us -> 89.4 us  [local(): pl.pallas_call(kernel, out_shape=shapes, in_specs=[hb, hb, hb, hb, sm, vm...]
where the time goes in v3:
time: 93.5 us; the launch traced here: 93.3 us
  Pallas kernels  91.9 us (98%)
  between operations  1.47 us (2%)
    pallas_call x1, Pallas kernels, local(): pl.pallas_call(kernel, out_shape=shapes, in_specs=[hb, hb, hb, hb, sm, vm...  89.4 us
    pallas_call x1, Pallas kernels, local(): pl.pallas_call(hand_over, out_shape=shapes, in_specs=[sm, vm, vm, vm, vm]...  2.46 us

profile of v3, /device:TPU:1, one launch (start us, length us, event | category | flops | bytes accessed | tf_op | source)
XLA Modules:
  0.0 93.3 jit_solution(13000391897304017106)
XLA Ops:
  1.3 89.4 %contrastive.1 = (f32[1]{0:T(128)}, bf16[128,1024]{1,0:T(8,128)(2,1)}, bf16[128,1024]{1,0:T(8,128)(2,1)}, f32[4,512]{1,0:T(4,128)}, f32[4,512]{1,0:T(4,128)}) custom-call(bf16[128,1024]{1,0:T(8,128)(2,1)} %sar_in.1, bf16[128,1024]{1,0:T(8,128)(2,1)} %opt_in.1, bf16[1024,512]{1,0:T(8,128)(2,1)} %ws_in.1, bf16[1024,512]{1,0:T(8,128)(2,1)} %wo_in.1, ...), custom_call_target="tpu_custom_call" | custom-call | tf_op jit(solution)/shard_map/contrastive/pallas_call | solution.py:655
  90.7 2.5 %hand_over.1 = (f32[1]{0:T(128)}, bf16[128,1024]{1,0:T(8,128)(2,1)}, bf16[128,1024]{1,0:T(8,128)(2,1)}, f32[4,512]{1,0:T(4,128)}, f32[4,512]{1,0:T(4,128)}) custom-call(f32[1]{0:T(128)} %get-tuple-element.10.l_in, bf16[128,1024]{1,0:T(8,128)(2,1)} %get-tuple-element.11.a_in, bf16[128,1024]{1,0:T(8,128)(2,1)} %get-tuple-element.12.b_in, ...), custom_call_target="tpu_custom_call" | custom-call | tf_op jit(solution)/shard_map/hand_over/pallas_call | solution.py:665

commit v4 on v3

--- a/solution.py
+++ b/solution.py
@@ -585,7 +585,6 @@
     smsg = head_exchange(0, grs)
     lr_ref[4] = gather_loss(0, NX, x, lmsg)
     lmsg = [send(lr_ref.at[4], lr_ref.at[4 + NY - d], dev(dy=d)) for d in range(1, NY)]
-    smsg = head_first(0, smsg)
 
     for copy in p2a + p2b:
         copy.wait_recv()
@@ -594,6 +593,7 @@
         gh1 = gh1 + p2h1_ref[d].astype(f32)
     gro = unproject(jnp.concatenate([gh0.T, gh1.T], axis=1), rawo_ref, inv_o)
     omsg = head_exchange(1, gro)
+    smsg = head_first(0, smsg)
     omsg = head_first(1, omsg)
     gsar_ref[...] = dot_nt(grs, ws_ref[...]).astype(bf16)
     gopt_ref[...] = dot_nt(gro, wo_ref[...]).astype(bf16)

time: 93.5 us -> 95 us (1.016)
  Pallas kernels: 91.9 us -> 93.3 us
    pallas_call x1, Pallas kernels: 89.4 us -> 90.9 us  [local(): pl.pallas_call(kernel, out_shape=shapes, in_specs=[hb, hb, hb, hb, sm, vm...]
where the time goes in v4:
time: 95 us; the launch traced here: 94.8 us
  Pallas kernels  93.3 us (98%)
  between operations  1.47 us (2%)
    pallas_call x1, Pallas kernels, local(): pl.pallas_call(kernel, out_shape=shapes, in_specs=[hb, hb, hb, hb, sm, vm...  90.9 us
    pallas_call x1, Pallas kernels, local(): pl.pallas_call(hand_over, out_shape=shapes, in_specs=[sm, vm, vm, vm, vm]...  2.46 us

profile of v4, /device:TPU:1, one launch (start us, length us, event | category | flops | bytes accessed | tf_op | source)
XLA Modules:
  0.0 94.8 jit_solution(18163745850248630416)
XLA Ops:
  1.3 90.9 %contrastive.1 = (f32[1]{0:T(128)}, bf16[128,1024]{1,0:T(8,128)(2,1)}, bf16[128,1024]{1,0:T(8,128)(2,1)}, f32[4,512]{1,0:T(4,128)}, f32[4,512]{1,0:T(4,128)}) custom-call(bf16[128,1024]{1,0:T(8,128)(2,1)} %sar_in.1, bf16[128,1024]{1,0:T(8,128)(2,1)} %opt_in.1, bf16[1024,512]{1,0:T(8,128)(2,1)} %ws_in.1, bf16[1024,512]{1,0:T(8,128)(2,1)} %wo_in.1, ...), custom_call_target="tpu_custom_call" | custom-call | tf_op jit(solution)/shard_map/contrastive/pallas_call | solution.py:655
  92.2 2.5 %hand_over.1 = (f32[1]{0:T(128)}, bf16[128,1024]{1,0:T(8,128)(2,1)}, bf16[128,1024]{1,0:T(8,128)(2,1)}, f32[4,512]{1,0:T(4,128)}, f32[4,512]{1,0:T(4,128)}) custom-call(f32[1]{0:T(128)} %get-tuple-element.10.l_in, bf16[128,1024]{1,0:T(8,128)(2,1)} %get-tuple-element.11.a_in, bf16[128,1024]{1,0:T(8,128)(2,1)} %get-tuple-element.12.b_in, ...), custom_call_target="tpu_custom_call" | custom-call | tf_op jit(solution)/shard_map/hand_over/pallas_call | solution.py:665
